TPU v7x, 512 devices: a whole 4x4x16 slice. The times are simulated.
512 devices in a mesh: tm: 64 (over x, z), row: 4 (over y), col: 2 (over core).
Axes of the slice: x: 4, y: 4, z: 16, core: 2. Of those that a mesh axis runs over, the one named last changes fastest.
Arguments:
- inputs: bfloat16 [64, 64, 64, 128], P('tm', 'row', 'col'), may hold values from -6 to 6
- cotangent: bfloat16 [64, 64, 64, 128], P('tm', 'row', 'col'), may hold values from -6 to 6
- w_in: bfloat16 [3, 3, 128, 256], replicated, may hold values from -0.1875 to 0.1875
- w_out: bfloat16 [3, 3, 256, 128], replicated, may hold values from -0.125 to 0.125
- decay: float32 [64, 256], P('tm'), may hold values from 0.35 to 1
- skip: float32 [128], replicated, may hold values from -1 to 1
Outputs:
- d_inputs: bfloat16 [64, 64, 64, 128], P('tm', 'row', 'col')
- d_in_conv: float32 [256, 3, 3, 128], P('tm')
- d_out_conv: float32 [256, 3, 3, 128], P('tm')
- decay_gradient: float32 [64, 256], P('tm')
All inputs are finite; a program needn't handle non-finite values.
Results may differ from a plain program's by a relative error of at most 0.017.
Values may be sent and summed in bfloat16 or wider, within the bound.
A program may use at most 192 MiB of HBM per device.

v0:
```python
import math

import jax
import jax.numpy as jnp
from jax import lax
from jax.sharding import PartitionSpec as P


def with_halo(cells, sides, width):
    for axis, dim in sides:
        count = lax.axis_size(axis)
        ends = count - 1
        head = lax.slice_in_dim(cells, 0, width, axis=dim)
        tail = lax.slice_in_dim(cells, cells.shape[dim] - width, cells.shape[dim], axis=dim)
        cells = jnp.concatenate(
            [
                lax.ppermute(tail, axis, [(i, (i + 1) % count) for i in range(ends)]),
                cells,
                lax.ppermute(head, axis, [((i + 1) % count, i) for i in range(ends)]),
            ],
            axis=dim,
        )
    return cells


def prefix(part, axis, combine, identity, reverse):
    count = lax.axis_size(axis)
    place = lax.axis_index(axis)
    ahead = count - 1 - place if reverse else place
    gathered = jax.tree.map(lambda a: lax.all_gather(a, axis), part)
    state = jax.tree.map(lambda a, e: jnp.zeros_like(a) + jnp.asarray(e, a.dtype), part, identity)

    def one(step, state):
        source = count - 1 - step if reverse else step
        return combine(
            state, jax.tree.map(lambda a: lax.dynamic_index_in_dim(a, source, 0, False), gathered)
        )

    return lax.fori_loop(0, ahead, one, state)


def tap_conv(padded, weight, rows, cols):
    total = None
    for di in range(3):
        for dj in range(3):
            piece = padded[:, di : di + rows, dj : dj + cols]
            term = jnp.einsum(
                "ftsi,io->ftso", piece, weight[di, dj], preferred_element_type=jnp.float32
            )
            total = term if total is None else total + term
    return total


def tap_conv_t(padded, weight, rows, cols):
    total = None
    for di in range(3):
        for dj in range(3):
            piece = padded[:, 2 - di : 2 - di + rows, 2 - dj : 2 - dj + cols]
            term = jnp.einsum(
                "ftsk,jk->ftsj", piece, weight[di, dj], preferred_element_type=jnp.float32
            )
            total = term if total is None else total + term
    return total


def combine_carry(preceding_snapshot, later):
    return (preceding_snapshot[0] * later[0], later[0] * preceding_snapshot[1] + later[1])


def body(inputs, cotangent, w_in, w_out, decay, skip):
    frames, rows, cols, feats = inputs.shape
    states = w_in.shape[3]
    whole = frames * lax.axis_size("tm") * rows * lax.axis_size("row") * cols * lax.axis_size("col")
    wscale = 1.0 / math.sqrt(whole)
    multiplier_adjoint = 1.0 / math.sqrt(rows * lax.axis_size("row") * cols * lax.axis_size("col"))
    rims = with_halo(jnp.stack([inputs, cotangent]), (("row", 2), ("col", 3)), 1)
    in_pad = rims[0]
    cot_pad = rims[1]
    source = tap_conv(in_pad, w_in, rows, cols)
    level = jnp.zeros((rows, cols, states), jnp.float32)
    factor = jnp.ones((states,), jnp.float32)
    level = decay[0] * level + source[0]
    factor = factor * decay[0]
    identity = (jnp.ones((states,), jnp.float32), jnp.zeros((rows, cols, states), jnp.float32))
    _, state_in = prefix((factor, level), "tm", combine_carry, identity, False)
    state_list = [level + factor * state_in]
    previous = jnp.stack([state_in] + state_list[:-1])
    state_all = jnp.stack(state_list)
    excite = tap_conv_t(cot_pad, w_out, rows, cols)
    local_adj = [None] * frames
    tails = [None] * frames
    local_adj[frames - 1] = excite[frames - 1]
    tails[frames - 1] = jnp.ones((states,), jnp.float32)
    summary = decay[0] * local_adj[0]
    _, adjoint_in = prefix((factor, summary), "tm", combine_carry, identity, True)
    adjoint = jnp.stack([local_adj[0] + tails[0] * adjoint_in])
    adjoint_b = adjoint.astype(jnp.bfloat16)
    adj_pad = with_halo(adjoint_b, (("row", 1), ("col", 2)), 1)
    grad_in = tap_conv_t(adj_pad, w_in, rows, cols)
    d_inputs = (grad_in + skip * cotangent.astype(jnp.float32)).astype(jnp.bfloat16)
    local_decay = multiplier_adjoint * jnp.sum(adjoint * previous, axis=(1, 2))
    decay_gradient = lax.psum(local_decay, ("row", "col"))
    state_b = state_all.astype(jnp.bfloat16)
    terms_in = []
    outgoing_terms = []
    for di in range(3):
        for dj in range(3):
            inp = in_pad[:, di : di + rows, dj : dj + cols]
            terms_in.append(
                jnp.einsum("ftsc,ftsp->pc", inp, adjoint_b, preferred_element_type=jnp.float32)
            )
            cot = cot_pad[:, 2 - di : 2 - di + rows, 2 - dj : 2 - dj + cols]
            outgoing_terms.append(
                jnp.einsum("ftsp,ftso->po", state_b, cot, preferred_element_type=jnp.float32)
            )
    incoming_term = jnp.stack(terms_in, axis=1).reshape(states, 3, 3, feats) * wscale
    term_out = jnp.stack(outgoing_terms, axis=1).reshape(states, 3, 3, feats) * wscale
    summed_in, summed_out = (
        lax.psum(incoming_term.astype(jnp.bfloat16), ("row", "col")).astype(jnp.float32),
        lax.psum(term_out.astype(jnp.bfloat16), ("row", "col")).astype(jnp.float32),
    )
    d_in_conv, d_out_conv = (
        lax.psum_scatter(summed_in, "tm", scatter_dimension=0, tiled=True),
        lax.psum_scatter(summed_out, "tm", scatter_dimension=0, tiled=True),
    )
    return (d_inputs, d_in_conv, d_out_conv, decay_gradient)


def solution(mesh):
    in_specs = (
        P("tm", "row", "col", None),
        P("tm", "row", "col", None),
        P(),
        P(),
        P("tm", None),
        P(),
    )
    out_specs = (
        P("tm", "row", "col", None),
        P("tm", None, None, None),
        P("tm", None, None, None),
        P("tm", None),
    )
    return jax.shard_map(body, mesh=mesh, in_specs=in_specs, out_specs=out_specs, check_vma=False)
```

profile of v0, /device:TPU:24, one launch (start us, length us, event | category | flops | bytes accessed | tf_op | source)
XLA Modules:
  0.0 1093.3 jit_solution(17285665557184551656)
XLA Ops:
  8.0 1.3 collective-permute-start
  9.3 4.5 collective-permute-start.1
  13.9 1.4 collective-permute-done.1
  16.1 1.3 collective-permute-start.2
  17.4 1.3 collective-permute-start.3
  18.7 1.8 collective-permute-done.3
  27.7 88.4 %all-gather.2 = f32[64,1,256]{2,1,0:T(1,128)S(1)} all-gather(f32[1,1,256]{2,1,0:T(1,128)S(1)} %bitcast.375), channel_id=1, replica_groups=mesh['tm'=64,'row'=4,'col'=2] {'tm'}, dimensions={0}, use_global_device_ids=true | all-gather | bytes 66560 | tf_op jit(solution)/shard_map/all_gather | solution.py:30
  116.2 1.3 dynamic-slice
  118.1 206.8 %all-gather.6.cloned.1.call-done = f32[1024,32,256]{2,1,0:T(8,128)} async-done(((f32[16,32,256]{2,1,0:T(8,128)}), f32[1024,32,256]{2,1,0:T(8,128)}) %all-gather.6.cloned.1.call-update) | async-done | bytes 33554448 | tf_op jit(solution)/shard_map/all_gather | solution.py:30
  325.0 82.0 %while.26 = (s32[]{:T(128)}, f32[16,32,256]{2,1,0:T(8,128)S(1)}, s32[]{:T(128)}, f32[64,256]{1,0:T(8,128)S(1)}, f32[64,16,32,256]{3,2,1,0:T(8,128)}, /*index=5*/s32[]{:T(128)}, s32[]{:T(128)}, s32[]{:T(128)}, s32[]{:T(128)}) while((s32[]{:T(128)}, f32[16,32,256]{2,1,0:T(8,128)S(1)}, s32[]{:T(128)}, f32[64,256]{1,0:T(8,128)S(1)}, ...), condition=%wide.region_1.2_spmd, body=%wide.region_0.1_spmd.sunk | while | flops 262150 | bytes 1576083 | solution.py:39
  325.0 1.3 bitcast_add_fusion.4
  326.3 1.3 bitcast_add_fusion.4
  327.6 1.3 bitcast_add_fusion.4
  328.9 1.3 bitcast_add_fusion.4
  330.2 1.3 bitcast_add_fusion.4
  331.5 1.3 bitcast_add_fusion.4
  332.8 1.3 bitcast_add_fusion.4
  334.1 1.3 bitcast_add_fusion.4
  335.4 1.3 bitcast_add_fusion.4
  336.7 1.3 bitcast_add_fusion.4
  338.0 1.3 bitcast_add_fusion.4
  339.3 1.3 bitcast_add_fusion.4
  340.6 1.3 bitcast_add_fusion.4
  342.0 1.3 bitcast_add_fusion.4
  343.3 1.3 bitcast_add_fusion.4
  344.5 1.3 bitcast_add_fusion.4
  345.8 1.3 bitcast_add_fusion.4
  347.1 1.3 bitcast_add_fusion.4
  348.5 1.3 bitcast_add_fusion.4
  352.4 1.3 bitcast_add_fusion.4
  353.7 1.3 bitcast_add_fusion.4
  356.3 1.3 bitcast_add_fusion.4
  357.6 1.3 bitcast_add_fusion.4
  360.2 1.3 bitcast_add_fusion.4
  361.5 1.3 bitcast_add_fusion.4
  364.1 1.3 bitcast_add_fusion.4
  365.4 1.3 bitcast_add_fusion.4
  369.3 1.3 bitcast_add_fusion.4
  370.6 1.3 bitcast_add_fusion.4
  373.2 1.3 bitcast_add_fusion.4
  374.5 1.3 bitcast_add_fusion.4
  378.4 1.3 bitcast_add_fusion.4
  381.0 1.3 bitcast_add_fusion.4
  382.3 1.3 bitcast_add_fusion.4
  383.6 1.3 bitcast_add_fusion.4
  386.2 1.3 bitcast_add_fusion.4
  387.5 1.3 bitcast_add_fusion.4
  390.1 1.3 bitcast_add_fusion.4
  392.7 1.3 bitcast_add_fusion.4
  394.0 1.3 bitcast_add_fusion.4
  395.3 1.3 bitcast_add_fusion.4
  396.6 1.3 bitcast_add_fusion.4
  397.9 1.3 bitcast_add_fusion.4
  399.2 1.3 bitcast_add_fusion.4
  400.5 1.3 bitcast_add_fusion.4
  401.8 1.3 bitcast_add_fusion.4
  407.0 211.8 %all-gather.8.cloned.1.call-done = f32[1024,32,256]{2,1,0:T(8,128)} async-done(((f32[16,32,256]{2,1,0:T(8,128)}), f32[1024,32,256]{2,1,0:T(8,128)}) %all-gather.8.cloned.1.call-update) | async-done | bytes 33554448 | tf_op jit(solution)/shard_map/all_gather | solution.py:30
  627.0 2.7 collective-permute-start.5
  629.7 1.3 collective-permute-start.4
  631.1 11.7 %psum.23 = f32[1,256]{1,0:T(1,128)} all-reduce(f32[1,256]{1,0:T(1,128)S(1)} %bitcast.377), channel_id=1, replica_groups=mesh['tm'=64,'row'=4,'col'=2] {'row','col'}, use_global_device_ids=true, to_apply=%region_9.10 | all-reduce | flops 256 | bytes 2048 | tf_op jit(solution)/shard_map/psum | solution.py:102
  642.8 1.3 collective-permute-start.6
  644.1 3.0 collective-permute-start.7
  650.9 128.6 %all-reduce.7.cloned.1.call-done = (bf16[256,3,3,128]{3,0,2,1:T(8,128)(2,1)}, bf16[256,3,3,128]{3,0,2,1:T(8,128)(2,1)}) async-done(((bf16[256,3,3,128]{3,0,2,1:T(8,128)(2,1)}, bf16[256,3,3,128]{3,0,2,1:T(8,128)(2,1)}), (bf16[256,3,3,128]{3,0,2,1:T(8,128)(2,1)}, bf16[256,3,3,128]{3,0,2,1:T(8,128)(2,1)})) %all-reduce.7.cloned.1.call-update) | async-done | bytes 1179664 | tf_op jit(solution)/shard_map/psum | solution.py:119
  779.5 306.6 %all-reduce.8 = (f32[256,3,3,128]{3,0,2,1:T(8,128)S(1)}, f32[256,3,3,128]{3,0,2,1:T(8,128)S(1)}) all-reduce(bf16[256,3,3,128]{3,0,2,1:T(8,128)(2,1)} %get-tuple-element.156, bf16[256,3,3,128]{3,0,2,1:T(8,128)(2,1)} %get-tuple-element.157), channel_id=4, replica_groups=mesh['tm'=64,'row'=4,'col'=2] {'tm'}, use_global_device_ids=true, to_apply=%region_3.4.clone | all-reduce | flops 589824 | bytes 3538944
  (166 shorter events, 43.2 us)
Async XLA Ops:
  7.2 14.5 %copy-start.3 = (bf16[3,3,256,128]{3,2,1,0:T(8,128)(2,1)S(1)}, bf16[3,3,256,128]{3,2,1,0:T(8,128)(2,1)}, u32[]{:S(2)}) copy-start(bf16[3,3,256,128]{3,2,1,0:T(8,128)(2,1)} %param.13) | copy-start | bytes 1769476
  7.2 317.8 %all-gather.6.cloned.1.call-start = ((), (), s32[]{:S(2)}) async-start(), calls=%async_computation | async-start | bytes 34078720 | tf_op jit(solution)/shard_map/all_gather | solution.py:30
  8.0 5.8 collective-permute-start
  9.3 6.0 collective-permute-start.1
  16.1 2.6 collective-permute-start.2
  17.4 3.1 collective-permute-start.3
  23.1 0.7 copy-start.4
  23.6 1.3 copy-start.1
  24.8 593.9 %all-gather.8.cloned.1.call-start = ((), (), s32[]{:S(2)}) async-start(), calls=%async_computation.1 | async-start | bytes 34078720 | tf_op jit(solution)/shard_map/all_gather | solution.py:30
  27.7 751.8 %all-reduce.7.cloned.1.call-start = ((), (), s32[]{:S(2)}) async-start(), calls=%async_computation.2 | async-start | bytes 2359296 | tf_op jit(solution)/shard_map/psum | solution.py:119
  618.8 1.0 copy-start
  627.0 15.7 %collective-permute-start.5 = (bf16[1,1,32,256]{3,2,1,0:T(8,128)(2,1)S(1)}, bf16[1,1,32,256]{3,2,1,0:T(8,128)(2,1)S(1)}, u32[]{:S(2)}, u32[]{:S(2)}) collective-permute-start(bf16[1,1,32,256]{3,2,1,0:T(8,128)(2,1)S(1)} %get-tuple-element.170), channel_id=1, source_target_pairs={{2,0},{4,2},{6,4},{3,1},{5,3},{7,5},{10,8},{12,10},{14,12},{11,9},... | collective-permute-start | bytes 49160 | tf_op jit(solution)/shard_map/ppermute | solution.py:19
  629.7 13.0 %collective-permute-start.4 = (bf16[1,1,32,256]{3,2,1,0:T(8,128)(2,1)S(1)}, bf16[1,1,32,256]{3,2,1,0:T(8,128)(2,1)S(1)}, u32[]{:S(2)}, u32[]{:S(2)}) collective-permute-start(bf16[1,1,32,256]{3,2,1,0:T(8,128)(2,1)S(1)} %get-tuple-element.169), channel_id=1, source_target_pairs={{0,2},{2,4},{4,6},{1,3},{3,5},{5,7},{8,10},{10,12},{12,14},{9,11},... | collective-permute-start | bytes 49160 | tf_op jit(solution)/shard_map/ppermute | solution.py:17
  642.8 4.6 collective-permute-start.6
  644.1 3.9 collective-permute-start.7
  649.1 0.9 copy-start.2
  649.1 0.9 copy-start.5
Sparse Core Ops, SparseCore 0:
  25.0 299.9 all-gather.5
  327.9 290.8 all-gather.7
  631.2 148.2 all-reduce.6
where the time goes:
time: 1100 us; the launch traced here: 1090 us
  waiting for transfers between devices  551 us (50%)
  blocking collectives  407 us (37%)
  other arithmetic  84.4 us (8%)
  starting transfers between devices  16.9 us (2%)
  between operations  14.9 us (1%)
  matrix products  13.1 us (1%)
    all_gather x2, waiting for transfers between devices, prefix(): gathered = jax.tree.map(lambda a: lax.all_gather(a, axis), part)  419 us
    unnamed x1, blocking collectives  307 us
    psum x1, waiting for transfers between devices, body(): lax.psum(incoming_term.astype(jnp.bfloat16), ('row', 'col'))  129 us
    all_gather x1, blocking collectives, prefix(): gathered = jax.tree.map(lambda a: lax.all_gather(a, axis), part)  88.4 us
    add x63, other arithmetic, combine_carry(): later[0] * preceding_snapshot[1] + later[1]  79.2 us
  transfers between devices with their start and end apart: 11, of which 6 were waited for; matrix products, arithmetic and copies ran while one was open for 8% of the time, Pallas kernels for 0%

commit v1 on v0

v1 whole, which is shorter than its diff:
```python
import functools
import math

import jax
import jax.numpy as jnp
from jax import lax
from jax.experimental import pallas as pl
from jax.experimental.pallas import tpu as pltpu
from jax.sharding import PartitionSpec as P

MESH = pl.DeviceIdType.MESH
F32 = jnp.float32
BF16 = jnp.bfloat16
X_CHIPS = 4
TAPS = [(di, dj) for di in range(3) for dj in range(3)]
SIDES = [(dr, dc) for dr in (-1, 0, 1) for dc in (-1, 0, 1) if dr or dc]


def dot(a, b, dims):
    return lax.dot_general(a, b, (dims, ((), ())), preferred_element_type=F32)


def exact_dot(a, b, dims):
    high = a.astype(BF16)
    rest = a - high.astype(F32)
    mid = rest.astype(BF16)
    low = (rest - mid.astype(F32)).astype(BF16)
    return dot(high, b, dims) + dot(mid, b, dims) + dot(low, b, dims)


def kernel(
    nx, nz, ny, rows, ln, wscale, dscale,
    in_ref, cot_ref, win_ref, wout_ref, dec_ref, skip_ref,
    dinp_ref, din_ref, dout_ref, dg_ref,
    t32, send_c, send_i, send_d, recv_c, recv_i, recv_d, dec_in, decp,
    pad_c, pad_i, pad_a, cols_c, cols_i, w_src, w_exc, w_back,
    exc, src,
    carry_a, carries_a, carry_s, carries_s, entry, dg_part,
    grad, grad_b, from_core, part_b, from_y, part_y, part_yb, from_x,
    mail, from_z, share, shares,
    p1_send, p1_recv, halo_send, halo_recv, car_send, car_recv,
    core_sem, y_send, y_recv, x_send, x_recv, ag_send, ag_recv,
):
    cells = 2 * rows
    wide = 2 * nz
    states = 2 * ln
    block = cells * nz
    tm = lax.axis_index("tm")
    y = lax.axis_index("row")
    c = lax.axis_index("col")
    x = tm // nz
    z = tm % nz
    q = 2 * z + c
    home = q // nz
    place = q % nz
    paired = home == c
    spot = 2 * y + c

    def here(dr, dc):
        return (y + dr >= 0) & (y + dr < ny) & (q + dc >= 0) & (q + dc < wide)

    def beside(dr, dc):
        to = q + dc
        return (x * nz + to // 2, y + dr, to % 2)

    def spot_id(o):
        to = (spot + o) % (2 * ny)
        return (tm, to // 2, to % 2)

    pad_c[...] = jnp.zeros_like(pad_c)
    pad_i[...] = jnp.zeros_like(pad_i)
    pad_a[...] = jnp.zeros_like(pad_a)

    barrier = pltpu.get_barrier_semaphore()

    def greet(device):
        pl.semaphore_signal(barrier, inc=1, device_id=device, device_id_type=MESH)

    @pl.loop(0, nz)
    def _(t):
        @pl.when(jnp.logical_not(paired & (t == z)))
        def _():
            greet((x * nz + t, y, home))

    beside_count = jnp.int32(0)
    for dr, dc in SIDES:
        beside_count += here(dr, dc).astype(jnp.int32)

        @pl.when(here(dr, dc))
        def _():
            greet(beside(dr, dc))

    for o in range(1, nx):
        greet((((x + o) % nx) * nz + z, y, c))
    for o in range(1, 2 * ny):
        greet(spot_id(o))

    def pack(ref, out):
        t32[...] = ref[...].astype(F32).reshape(block, ln)

        @pl.loop(0, nz)
        def _(k):
            for col in range(2):
                out[k, col * rows : (col + 1) * rows] = t32[
                    pl.ds(2 * k + col, rows, stride=wide)
                ].astype(BF16)

    def scatter(at, source, target):
        @pl.loop(0, nz)
        def _(o):
            k = (z + o) % nz
            to = c * nz + k

            @pl.when(to == q)
            def _():
                pltpu.make_async_copy(source(k), target.at[z], p1_recv.at[at]).start()

            @pl.when(to != q)
            def _():
                pltpu.make_async_remote_copy(
                    source(k), target.at[z], p1_send.at[at], p1_recv.at[at],
                    device_id=(x * nz + to // 2, y, to % 2), device_id_type=MESH,
                ).start()

    def give_back(at, source, target):
        @pl.loop(0, nz)
        def _(o):
            t = (z + o) % nz
            own = paired & (t == z)

            @pl.when(own)
            def _():
                pltpu.make_async_copy(source.at[t], target.at[place], p1_recv.at[at]).start()

            @pl.when(jnp.logical_not(own))
            def _():
                pltpu.make_async_remote_copy(
                    source.at[t], target.at[place], p1_send.at[at], p1_recv.at[at],
                    device_id=(x * nz + t, y, home), device_id_type=MESH,
                ).start()

    def arrived(at, target):
        pltpu.make_async_copy(target, target, p1_recv.at[at]).wait()

    def sent(at, like):
        @pl.when(paired)
        def _():
            part = like.at[pl.ds(0, nz - 1)]
            pltpu.make_async_copy(part, part, p1_send.at[at]).wait()

        @pl.when(jnp.logical_not(paired))
        def _():
            pltpu.make_async_copy(like, like, p1_send.at[at]).wait()

    pack(cot_ref, send_c)
    pl.semaphore_wait(
        barrier, nz - paired.astype(jnp.int32) + beside_count + (nx - 1) + (2 * ny - 1)
    )
    scatter(0, lambda k: dec_ref, dec_in)
    scatter(1, lambda k: send_c.at[k], recv_c)
    pack(in_ref, send_i)
    scatter(2, lambda k: send_i.at[k], recv_i)

    old = lax.broadcasted_iota(jnp.int32, (states, states), 0)
    new = lax.broadcasted_iota(jnp.int32, (states, states), 1)
    perm = jnp.where((old % ny) * (nx * nz) + old // ny == new, 1.0, 0.0).astype(BF16)

    @pl.loop(0, 9)
    def _(tap):
        at = pl.ds(pl.multiple_of(tap * ln, ln), ln)
        w_src[at] = dot(win_ref[tap], perm, ((1,), (0,))).astype(BF16)
        w_exc[at] = dot(wout_ref[tap], perm, ((0,), (0,))).astype(BF16)
        w_back[tap] = dot(perm, win_ref[tap], ((0,), (1,))).astype(BF16)

    arrived(0, dec_in)
    rates = exact_dot(dec_in[...].reshape(nz, states), perm, ((1,), (0,)))
    decp[0] = rates[:, :ln]
    decp[1] = rates[:, ln:]

    def unpack(recv, pad):
        t32[...] = recv[...].astype(F32).reshape(block, ln)

        @pl.loop(0, rows)
        def _(r):
            for col in range(2):
                pad[1 + col, 1 + r] = t32[
                    pl.ds(col * rows + r, nz, stride=cells)
                ].astype(BF16)

    def halo(which, pad, act):
        for at, (dr, dc) in enumerate(SIDES):
            there = (-dr, -dc)
            from_rows = {-1: pl.ds(1, 1), 0: pl.ds(1, rows), 1: pl.ds(rows, 1)}[dr]
            to_rows = {-1: pl.ds(rows + 1, 1), 0: pl.ds(1, rows), 1: pl.ds(0, 1)}[dr]
            from_cols = {-1: pl.ds(1, 1), 0: pl.ds(1, 2), 1: pl.ds(2, 1)}[dc]
            to_cols = {-1: pl.ds(3, 1), 0: pl.ds(1, 2), 1: pl.ds(0, 1)}[dc]
            copy = pltpu.make_async_remote_copy(
                pad.at[from_cols, from_rows], pad.at[to_cols, to_rows],
                halo_send.at[which, at], halo_recv.at[which, at],
                device_id=beside(dr, dc), device_id_type=MESH,
            )
            if act == "send":
                pl.when(here(dr, dc))(copy.start)
            elif act == "sent":
                pl.when(here(dr, dc))(copy.wait_send)
            else:
                pl.when(here(*there))(copy.wait_recv)

    def lay_out(pad, cols, flip):
        for tap, (di, dj) in enumerate(TAPS):
            a, b = (2 - di, 2 - dj) if flip else (di, dj)
            cols[:, tap * ln : (tap + 1) * ln] = pad[b : b + 2, a : a + rows].reshape(block, ln)

    def carry_copy(send, recv, which, to):
        return pltpu.make_async_remote_copy(
            send, recv.at[x], car_send.at[which, to], car_recv.at[which, x],
            device_id=(to * nz + z, y, c), device_id_type=MESH,
        )

    def carry_from(recv, which, source):
        return pltpu.make_async_copy(recv.at[source], recv.at[source], car_recv.at[which, source])

    def fold(recv, which, order, needed):
        entry[...] = jnp.zeros_like(entry)
        for source in order:
            @pl.when(needed(source))
            def _():
                carry_from(recv, which, source).wait()
                for h in range(2):
                    entry[h] = (
                        recv[source, h, :cells] + recv[source, h, cells : cells + 1] * entry[h]
                    )

    frame = lambda t: pl.ds(t, cells, stride=nz)

    arrived(1, recv_c)
    unpack(recv_c, pad_c)
    halo(0, pad_c, "send")
    halo(0, pad_c, "arrive")
    lay_out(pad_c, cols_c, True)
    value = dot(cols_c[...], w_exc[...], ((1,), (0,)))
    exc[0] = value[:, :ln]
    exc[1] = value[:, ln:]

    for h in range(2):
        def adjoint_step(i, held):
            b, factor = held
            t = nz - 1 - i
            rate = decp[h, pl.ds(t, 1)]
            return rate * (exc[h, frame(t)] + b), factor * rate

        b, factor = lax.fori_loop(
            0, nz, adjoint_step, (jnp.zeros((cells, ln), F32), jnp.ones((1, ln), F32))
        )
        carry_a[h, :cells] = b
        carry_a[h, cells:] = jnp.broadcast_to(factor, (8, ln))
    for to in range(nx):
        pl.when(to < x)(carry_copy(carry_a, carries_a, 0, to).start)

    arrived(2, recv_i)
    unpack(recv_i, pad_i)
    halo(1, pad_i, "send")

    fold(carries_a, 0, range(nx - 1, -1, -1), lambda source: source > x)
    for h in range(2):
        def adjoint_final(i, b):
            t = nz - 1 - i
            level = exc[h, frame(t)] + b
            exc[h, frame(t)] = level
            return decp[h, pl.ds(t, 1)] * level

        lax.fori_loop(0, nz, adjoint_final, entry[h])
    adjoint_b = jnp.concatenate([exc[0], exc[1]], axis=1).astype(BF16)
    pad_a[1:3, 1 : 1 + rows] = adjoint_b.reshape(2, rows, nz, states)
    halo(2, pad_a, "send")

    halo(1, pad_i, "arrive")
    lay_out(pad_i, cols_i, False)
    value = dot(cols_i[...], w_src[...], ((1,), (0,)))
    src[0] = value[:, :ln]
    src[1] = value[:, ln:]
    for h in range(2):
        def state_step(t, level):
            return decp[h, pl.ds(t, 1)] * level + src[h, frame(t)]

        carry_s[h, :cells] = lax.fori_loop(0, nz, state_step, jnp.zeros((cells, ln), F32))
        carry_s[h, cells:] = carry_a[h, cells:]
    for to in range(nx):
        pl.when(to > x)(carry_copy(carry_s, carries_s, 1, to).start)

    def core_copy():
        return pltpu.make_async_remote_copy(
            grad_b, from_core, core_sem.at[0], core_sem.at[1],
            device_id=(tm, y, 1 - c), device_id_type=MESH,
        )

    grad[0] = dot(
        pad_a[1:3, 1 : 1 + rows].reshape(block, states), cols_i[...], ((0,), (0,))
    ).reshape(grad.shape[1:])

    @pl.when(c == 1)
    def _():
        grad_b[...] = grad[0].astype(BF16)
        core_copy().start()

    halo(2, pad_a, "arrive")
    total = skip_ref[...] * pad_c[1:3, 1 : 1 + rows].reshape(block, ln).astype(F32)
    for tap, (di, dj) in enumerate(TAPS):
        a, b = 2 - di, 2 - dj
        total += dot(pad_a[b : b + 2, a : a + rows].reshape(block, states), w_back[tap], ((1,), (0,)))
    t32[...] = total

    @pl.loop(0, nz)
    def _(t):
        send_d[t] = t32[frame(t)].astype(BF16)

    give_back(3, send_d, recv_d)

    fold(carries_s, 1, range(nx), lambda source: source < x)
    for h in range(2):
        def state_final(t, level):
            now = decp[h, pl.ds(t, 1)] * level + src[h, frame(t)]
            src[h, frame(t)] = now
            dg_part[h, pl.ds(t, 1)] = jnp.sum(exc[h, frame(t)] * level, axis=0, keepdims=True)
            return now

        lax.fori_loop(0, nz, state_final, entry[h])
    state_b = jnp.concatenate([src[0], src[1]], axis=1).astype(BF16)
    grad[1] = dot(state_b, cols_c[...], ((0,), (0,))).reshape(grad.shape[1:])

    @pl.when(c == 0)
    def _():
        grad_b[...] = grad[1].astype(BF16)
        core_copy().start()

    core_copy().wait_recv()

    def y_copy(o):
        to = (y + o) % ny
        return pltpu.make_async_remote_copy(
            part_b.at[to], from_y.at[o - 1], y_send.at[o - 1], y_recv.at[o - 1],
            device_id=(tm, to, c), device_id_type=MESH,
        )

    part_b[...] = (grad[c] + from_core[...].astype(F32)).astype(BF16)
    for o in range(1, ny):
        y_copy(o).start()

    arrived(3, recv_d)
    t32[...] = recv_d[...].astype(F32).reshape(block, ln)

    @pl.loop(0, rows)
    def _(r):
        dinp_ref[r] = t32[pl.ds(r, wide, stride=rows)].astype(BF16)

    dg_old = exact_dot(
        jnp.concatenate([dg_part[0], dg_part[1]], axis=1), perm, ((1,), (1,))
    )
    mail[:, 9] = dg_old[:, :ln]
    mail[:, 10] = dg_old[:, ln:]

    summed = grad[c, y] + from_core[y].astype(F32)
    for o in range(1, ny):
        y_copy(o).wait_recv()
        summed += from_y[o - 1].astype(F32)
    part_y[...] = summed.reshape(part_y.shape)
    part_yb[...] = summed.astype(BF16).reshape(part_y.shape)

    def x_copy(o):
        to = (x + o) % nx
        return pltpu.make_async_remote_copy(
            part_yb.at[to], from_x.at[o - 1], x_send.at[o - 1], x_recv.at[o - 1],
            device_id=(to * nz + z, y, c), device_id_type=MESH,
        )

    for o in range(1, nx):
        x_copy(o).start()
    summed = part_y[x]
    for o in range(1, nx):
        x_copy(o).wait_recv()
        summed += from_x[o - 1].astype(F32)
    for tap in range(9):
        mail[:, tap] = summed[:, tap * ln : (tap + 1) * ln]

    give_back(4, mail, from_z)
    arrived(4, from_z)
    both = [jnp.zeros((11, ln), F32), jnp.zeros((11, ln), F32)]
    for k in range(nz):
        both[k % 2] = both[k % 2] + from_z[k]
    share[:9] = both[0][:9]
    share[9:18] = both[1][:9]
    share[18:20] = both[0][9:] + both[1][9:]

    def share_copy(o):
        return pltpu.make_async_remote_copy(
            share, shares.at[spot], ag_send.at[o - 1], ag_recv.at[o - 1],
            device_id=spot_id(o), device_id_type=MESH,
        )

    for o in range(1, 2 * ny):
        share_copy(o).start()
    shares[spot] = share[...]
    for o in range(1, 2 * ny):
        share_copy(o).wait_recv()
    for j in range(ny):
        din_ref[j] = (shares[2 * j, :9] + shares[2 * j + 1, :9]) * wscale
        dout_ref[j] = (shares[2 * j, 9:18] + shares[2 * j + 1, 9:18]) * wscale
    total = shares[0, 18:20]
    for s in range(1, 2 * ny):
        total += shares[s, 18:20]
    dg_ref[...] = total * dscale

    sent(0, dec_in)
    sent(1, send_c)
    sent(2, send_i)
    sent(3, send_d)
    sent(4, mail)
    for which, pad in enumerate((pad_c, pad_i, pad_a)):
        halo(which, pad, "sent")
    for to in range(nx):
        pl.when(to < x)(carry_copy(carry_a, carries_a, 0, to).wait_send)
        pl.when(to > x)(carry_copy(carry_s, carries_s, 1, to).wait_send)
    core_copy().wait_send()
    for o in range(1, ny):
        y_copy(o).wait_send()
    for o in range(1, nx):
        x_copy(o).wait_send()
    for o in range(1, 2 * ny):
        share_copy(o).wait_send()


def body(nx, inputs, cotangent, w_in, w_out, decay, skip):
    _, rows, wide, ln = inputs.shape
    ny = lax.axis_size("row")
    nz = lax.axis_size("tm") // nx
    states = w_in.shape[3]
    cells = 2 * rows
    block = cells * nz
    wscale = 1.0 / math.sqrt(nx * nz * ny * rows * wide * 2)
    dscale = 1.0 / math.sqrt(ny * rows * wide * 2)
    vmem = pltpu.VMEM
    dma = pltpu.SemaphoreType.DMA
    scratch = [
        vmem((block, ln), F32),
        vmem((nz, cells, ln), BF16),
        vmem((nz, cells, ln), BF16),
        vmem((nz, cells, ln), BF16),
        vmem((nz, cells, ln), BF16),
        vmem((nz, cells, ln), BF16),
        vmem((nz, cells, ln), BF16),
        vmem((nz, 1, states), F32),
        vmem((2, nz, ln), F32),
        vmem((4, rows + 2, nz, ln), BF16),
        vmem((4, rows + 2, nz, ln), BF16),
        vmem((4, rows + 2, nz, states), BF16),
        vmem((block, 9 * ln), BF16),
        vmem((block, 9 * ln), BF16),
        vmem((9 * ln, states), BF16),
        vmem((9 * ln, states), BF16),
        vmem((9, states, ln), BF16),
        vmem((2, block, ln), F32),
        vmem((2, block, ln), F32),
        vmem((2, cells + 8, ln), F32),
        vmem((nx, 2, cells + 8, ln), F32),
        vmem((2, cells + 8, ln), F32),
        vmem((nx, 2, cells + 8, ln), F32),
        vmem((2, cells, ln), F32),
        vmem((2, nz, ln), F32),
        vmem((2, ny, nx * nz, 9 * ln), F32),
        vmem((ny, nx * nz, 9 * ln), BF16),
        vmem((ny, nx * nz, 9 * ln), BF16),
        vmem((ny, nx * nz, 9 * ln), BF16),
        vmem((ny - 1, nx * nz, 9 * ln), BF16),
        vmem((nx, nz, 9 * ln), F32),
        vmem((nx, nz, 9 * ln), BF16),
        vmem((nx - 1, nz, 9 * ln), BF16),
        vmem((nz, 11, ln), F32),
        vmem((nz, 11, ln), F32),
        vmem((20, ln), F32),
        vmem((2 * ny, 20, ln), F32),
        dma((5,)),
        dma((5,)),
        dma((3, 8)),
        dma((3, 8)),
        dma((2, nx)),
        dma((2, nx)),
        dma((2,)),
        dma((ny - 1,)),
        dma((ny - 1,)),
        dma((nx - 1,)),
        dma((nx - 1,)),
        dma((2 * ny - 1,)),
        dma((2 * ny - 1,)),
    ]
    d_inputs, d_in, d_out, d_decay = pl.pallas_call(
        functools.partial(kernel, nx, nz, ny, rows, ln, wscale, dscale),
        out_shape=(
            jax.ShapeDtypeStruct((rows, wide, ln), BF16),
            jax.ShapeDtypeStruct((ny, 9, ln), F32),
            jax.ShapeDtypeStruct((ny, 9, ln), F32),
            jax.ShapeDtypeStruct((2, ln), F32),
        ),
        in_specs=[pl.BlockSpec(memory_space=pltpu.VMEM)] * 6,
        out_specs=tuple([pl.BlockSpec(memory_space=pltpu.VMEM)] * 4),
        scratch_shapes=scratch,
        compiler_params=pltpu.CompilerParams(
            collective_id=0, has_side_effects=True, vmem_limit_bytes=48 * 1024 * 1024
        ),
        cost_estimate=pl.CostEstimate(
            flops=5 * 2 * block * 9 * ln * states, bytes_accessed=4 * 1024 * 1024, transcendentals=0
        ),
    )(
        inputs.reshape(rows, wide, ln),
        cotangent.reshape(rows, wide, ln),
        w_in.reshape(9, ln, states),
        w_out.reshape(9, states, ln),
        decay,
        skip.reshape(1, ln),
    )
    return (
        d_inputs[None],
        d_in.reshape(ny, 3, 3, ln),
        d_out.reshape(ny, 3, 3, ln),
        d_decay.reshape(1, states),
    )


def solution(mesh, nx=X_CHIPS):
    in_specs = (
        P("tm", "row", "col", None),
        P("tm", "row", "col", None),
        P(),
        P(),
        P("tm", None),
        P(),
    )
    out_specs = (
        P("tm", "row", "col", None),
        P("tm", None, None, None),
        P("tm", None, None, None),
        P("tm", None),
    )
    return jax.shard_map(
        functools.partial(body, nx), mesh=mesh, in_specs=in_specs, out_specs=out_specs,
        check_vma=False,
    )
```

time: 1100 us -> 80.8 us (0.07)
  the two profiles are of different devices: /device:TPU:24 before, /device:TPU:1 now
where the time goes in v1:
time: 80.8 us; the launch traced here: 80.6 us
  Pallas kernels  72.9 us (90%)
  local copies, waits for them, and re-layouts  7.05 us (9%)
    pallas_call x1, Pallas kernels, body(): pl.pallas_call(functools.partial(kernel, nx, nz, ny, rows, ln, wscale, ds...  72.9 us
    unnamed x14, local copies, waits for them, and re-layouts  5.82 us

profile of v1, /device:TPU:1, one launch (start us, length us, event | category | flops | bytes accessed | tf_op | source)
XLA Modules:
  0.0 80.6 jit_solution(5998315935818718578)
XLA Ops:
  0.6 0.0 copy-start.4
  0.6 0.0 copy-start.5
  0.7 0.7 copy-done.4
  1.3 0.0 copy-done.5
  1.3 0.0 copy-start
  1.3 1.1 %copy-done = bf16[3,3,128,256]{3,2,1,0:T(8,128)(2,1)S(1)} copy-done((bf16[3,3,128,256]{3,2,1,0:T(8,128)(2,1)S(1)}, bf16[3,3,128,256]{3,2,1,0:T(8,128)(2,1)}, u32[]{:S(2)}) %copy-start) | copy-done | bytes 589848
  2.4 0.0 copy-start.1
  2.4 1.1 %copy-done.1 = bf16[3,3,256,128]{3,2,1,0:T(8,128)(2,1)S(1)} copy-done((bf16[3,3,256,128]{3,2,1,0:T(8,128)(2,1)S(1)}, bf16[3,3,256,128]{3,2,1,0:T(8,128)(2,1)}, u32[]{:S(2)}) %copy-start.1) | copy-done | bytes 589848
  3.4 0.0 copy-start.2
  3.4 0.9 %copy-done.2 = bf16[1,16,32,128]{3,2,1,0:T(8,128)(2,1)S(1)} copy-done((bf16[1,16,32,128]{3,2,1,0:T(8,128)(2,1)S(1)}, bf16[1,16,32,128]{3,2,1,0:T(8,128)(2,1)}, u32[]{:S(2)}) %copy-start.2) | copy-done | bytes 131096
  4.3 0.0 copy-start.3
  4.4 0.9 %copy-done.3 = bf16[1,16,32,128]{3,2,1,0:T(8,128)(2,1)S(1)} copy-done((bf16[1,16,32,128]{3,2,1,0:T(8,128)(2,1)S(1)}, bf16[1,16,32,128]{3,2,1,0:T(8,128)(2,1)}, u32[]{:S(2)}) %copy-start.3) | copy-done | bytes 131096
  5.3 72.9 %shard_map.93 = (bf16[16,32,128]{2,1,0:T(8,128)(2,1)S(1)}, f32[4,9,128]{2,1,0:T(8,128)S(1)}, f32[4,9,128]{2,1,0:T(8,128)S(1)}, f32[2,128]{1,0:T(2,128)S(1)}) custom-call(bf16[16,32,128]{2,1,0:T(8,128)(2,1)S(1)} %bitcast.13, bf16[16,32,128]{2,1,0:T(8,128)(2,1)S(1)} %bitcast.14, bf16[9,128,256]{2,1,0:T(8,128)(2,1)S(1)} %bitcast.11, ...), custom_call_target="tpu_custom_call" | custom-call | flops 1509949440 | bytes 4194304 | tf_op jit(solution)/shard_map/pallas_call | solution.py:495
  78.1 0.6 copy.12
  78.7 0.6 copy.13
  79.4 0.7 copy.16
  80.0 0.6 copy.17
Async XLA Ops:
  0.6 0.7 copy-start.4
  0.6 0.7 copy-start.5
  1.3 1.1 %copy-start = (bf16[3,3,128,256]{3,2,1,0:T(8,128)(2,1)S(1)}, bf16[3,3,128,256]{3,2,1,0:T(8,128)(2,1)}, u32[]{:S(2)}) copy-start(bf16[3,3,128,256]{3,2,1,0:T(8,128)(2,1)} %param.8) | copy-start | bytes 1769476
  2.4 1.1 %copy-start.1 = (bf16[3,3,256,128]{3,2,1,0:T(8,128)(2,1)S(1)}, bf16[3,3,256,128]{3,2,1,0:T(8,128)(2,1)}, u32[]{:S(2)}) copy-start(bf16[3,3,256,128]{3,2,1,0:T(8,128)(2,1)} %param.9) | copy-start | bytes 1769476
  3.4 0.9 %copy-start.2 = (bf16[1,16,32,128]{3,2,1,0:T(8,128)(2,1)S(1)}, bf16[1,16,32,128]{3,2,1,0:T(8,128)(2,1)}, u32[]{:S(2)}) copy-start(bf16[1,16,32,128]{3,2,1,0:T(8,128)(2,1)} %param.6) | copy-start | bytes 393220
  4.3 0.9 %copy-start.3 = (bf16[1,16,32,128]{3,2,1,0:T(8,128)(2,1)S(1)}, bf16[1,16,32,128]{3,2,1,0:T(8,128)(2,1)}, u32[]{:S(2)}) copy-start(bf16[1,16,32,128]{3,2,1,0:T(8,128)(2,1)} %param.7) | copy-start | bytes 393220

commit v2 on v1

--- a/solution.py
+++ b/solution.py
@@ -29,17 +29,18 @@
 
 
 def kernel(
-    nx, nz, ny, rows, ln, wscale, dscale,
-    in_ref, cot_ref, win_ref, wout_ref, dec_ref, skip_ref,
-    dinp_ref, din_ref, dout_ref, dg_ref,
+    nx, nz, ny, rows, ln,
+    in_hbm, cot_hbm, win_hbm, wout_hbm, dec_hbm, skip_hbm,
+    dinp_hbm, shares,
+    in_ref, cot_ref, win_ref, wout_ref, dec_ref, skip_ref, fetch_sem,
     t32, send_c, send_i, send_d, recv_c, recv_i, recv_d, dec_in, decp,
     pad_c, pad_i, pad_a, cols_c, cols_i, w_src, w_exc, w_back,
     exc, src,
     carry_a, carries_a, carry_s, carries_s, entry, dg_part,
-    grad, grad_b, from_core, part_b, from_y, part_y, part_yb, from_x,
-    mail, from_z, share, shares,
+    grad, grad_b, from_core, part_b, from_xy,
+    mail32, mail, from_z, share, dinp_ref, put_sem,
     p1_send, p1_recv, halo_send, halo_recv, car_send, car_recv,
-    core_sem, y_send, y_recv, x_send, x_recv, ag_send, ag_recv,
+    core_sem, xy_send, xy_recv, ag_send, ag_recv,
 ):
     cells = 2 * rows
     wide = 2 * nz
@@ -55,6 +56,7 @@
     place = q % nz
     paired = home == c
     spot = 2 * y + c
+    flat = x * ny + y
 
     def here(dr, dc):
         return (y + dr >= 0) & (y + dr < ny) & (q + dc >= 0) & (q + dc < wide)
@@ -63,13 +65,23 @@
         to = q + dc
         return (x * nz + to // 2, y + dr, to % 2)
 
+    def flat_id(o):
+        to = (flat + o) % (nx * ny)
+        return ((to // ny) * nz + z, to % ny, c)
+
     def spot_id(o):
         to = (spot + o) % (2 * ny)
         return (tm, to // 2, to % 2)
 
-    pad_c[...] = jnp.zeros_like(pad_c)
-    pad_i[...] = jnp.zeros_like(pad_i)
-    pad_a[...] = jnp.zeros_like(pad_a)
+    fetches = [
+        pltpu.make_async_copy(source, target, fetch_sem.at[at])
+        for at, (source, target) in enumerate([
+            (cot_hbm, cot_ref), (in_hbm, in_ref), (dec_hbm, dec_ref),
+            (wout_hbm, wout_ref), (win_hbm, win_ref), (skip_hbm, skip_ref),
+        ])
+    ]
+    for fetch in fetches:
+        fetch.start()
 
     barrier = pltpu.get_barrier_semaphore()
 
@@ -82,6 +94,17 @@
         def _():
             greet((x * nz + t, y, home))
 
+    @pl.loop(1, nx * ny)
+    def _(o):
+        greet(flat_id(o))
+
+    for o in range(1, 2 * ny, 2):
+        greet((tm, (y + o // 2) % ny, 1 - c))
+
+    pad_c[...] = jnp.zeros_like(pad_c)
+    pad_i[...] = jnp.zeros_like(pad_i)
+    pad_a[...] = jnp.zeros_like(pad_a)
+
     beside_count = jnp.int32(0)
     for dr, dc in SIDES:
         beside_count += here(dr, dc).astype(jnp.int32)
@@ -90,10 +113,6 @@
         def _():
             greet(beside(dr, dc))
 
-    for o in range(1, nx):
-        greet((((x + o) % nx) * nz + z, y, c))
-    for o in range(1, 2 * ny):
-        greet(spot_id(o))
 
     def pack(ref, out):
         t32[...] = ref[...].astype(F32).reshape(block, ln)
@@ -152,14 +171,20 @@
         def _():
             pltpu.make_async_copy(like, like, p1_send.at[at]).wait()
 
+    fetches[0].wait()
     pack(cot_ref, send_c)
     pl.semaphore_wait(
-        barrier, nz - paired.astype(jnp.int32) + beside_count + (nx - 1) + (2 * ny - 1)
+        barrier, nz - paired.astype(jnp.int32) + beside_count + (nx * ny - 1) + ny
     )
+    scatter(1, lambda k: send_c.at[k], recv_c)
+    fetches[1].wait()
+    pack(in_ref, send_i)
+    fetches[2].wait()
     scatter(0, lambda k: dec_ref, dec_in)
-    scatter(1, lambda k: send_c.at[k], recv_c)
-    pack(in_ref, send_i)
     scatter(2, lambda k: send_i.at[k], recv_i)
+    fetches[3].wait()
+    fetches[4].wait()
+    fetches[5].wait()
 
     old = lax.broadcasted_iota(jnp.int32, (states, states), 0)
     new = lax.broadcasted_iota(jnp.int32, (states, states), 1)
@@ -298,23 +323,27 @@
         pad_a[1:3, 1 : 1 + rows].reshape(block, states), cols_i[...], ((0,), (0,))
     ).reshape(grad.shape[1:])
 
+    def xy_copy(o):
+        to = (flat + o) % (nx * ny)
+        return pltpu.make_async_remote_copy(
+            part_b.at[to % ny, to // ny], from_xy.at[o - 1], xy_send.at[o - 1], xy_recv.at[o - 1],
+            device_id=flat_id(o), device_id_type=MESH,
+        )
+
+    def begin():
+        core_copy().wait_recv()
+        part_b[...] = (grad[c] + from_core[...].astype(F32)).astype(BF16)
+
+        @pl.loop(1, nx * ny)
+        def _(o):
+            xy_copy(o).start()
+
     @pl.when(c == 1)
     def _():
         grad_b[...] = grad[0].astype(BF16)
         core_copy().start()
 
-    halo(2, pad_a, "arrive")
-    total = skip_ref[...] * pad_c[1:3, 1 : 1 + rows].reshape(block, ln).astype(F32)
-    for tap, (di, dj) in enumerate(TAPS):
-        a, b = 2 - di, 2 - dj
-        total += dot(pad_a[b : b + 2, a : a + rows].reshape(block, states), w_back[tap], ((1,), (0,)))
-    t32[...] = total
-
-    @pl.loop(0, nz)
-    def _(t):
-        send_d[t] = t32[frame(t)].astype(BF16)
-
-    give_back(3, send_d, recv_d)
+    pl.when(c == 0)(begin)
 
     fold(carries_s, 1, range(nx), lambda source: source < x)
     for h in range(2):
@@ -333,18 +362,20 @@
         grad_b[...] = grad[1].astype(BF16)
         core_copy().start()
 
-    core_copy().wait_recv()
-
-    def y_copy(o):
-        to = (y + o) % ny
-        return pltpu.make_async_remote_copy(
-            part_b.at[to], from_y.at[o - 1], y_send.at[o - 1], y_recv.at[o - 1],
-            device_id=(tm, to, c), device_id_type=MESH,
-        )
-
-    part_b[...] = (grad[c] + from_core[...].astype(F32)).astype(BF16)
-    for o in range(1, ny):
-        y_copy(o).start()
+    pl.when(c == 1)(begin)
+
+    halo(2, pad_a, "arrive")
+    total = skip_ref[...] * pad_c[1:3, 1 : 1 + rows].reshape(block, ln).astype(F32)
+    for tap, (di, dj) in enumerate(TAPS):
+        a, b = 2 - di, 2 - dj
+        total += dot(pad_a[b : b + 2, a : a + rows].reshape(block, states), w_back[tap], ((1,), (0,)))
+    t32[...] = total
+
+    @pl.loop(0, nz)
+    def _(t):
+        send_d[t] = t32[frame(t)].astype(BF16)
+
+    give_back(3, send_d, recv_d)
 
     arrived(3, recv_d)
     t32[...] = recv_d[...].astype(F32).reshape(block, ln)
@@ -353,43 +384,38 @@
     def _(r):
         dinp_ref[r] = t32[pl.ds(r, wide, stride=rows)].astype(BF16)
 
+    put_dinp = pltpu.make_async_copy(dinp_ref, dinp_hbm, put_sem.at[0])
+    put_dinp.start()
+
     dg_old = exact_dot(
         jnp.concatenate([dg_part[0], dg_part[1]], axis=1), perm, ((1,), (1,))
     )
-    mail[:, 9] = dg_old[:, :ln]
-    mail[:, 10] = dg_old[:, ln:]
-
-    summed = grad[c, y] + from_core[y].astype(F32)
-    for o in range(1, ny):
-        y_copy(o).wait_recv()
-        summed += from_y[o - 1].astype(F32)
-    part_y[...] = summed.reshape(part_y.shape)
-    part_yb[...] = summed.astype(BF16).reshape(part_y.shape)
-
-    def x_copy(o):
-        to = (x + o) % nx
-        return pltpu.make_async_remote_copy(
-            part_yb.at[to], from_x.at[o - 1], x_send.at[o - 1], x_recv.at[o - 1],
-            device_id=(to * nz + z, y, c), device_id_type=MESH,
-        )
-
-    for o in range(1, nx):
-        x_copy(o).start()
-    summed = part_y[x]
-    for o in range(1, nx):
-        x_copy(o).wait_recv()
-        summed += from_x[o - 1].astype(F32)
+    high = dg_old.astype(BF16).astype(F32)
+    mid = (dg_old - high).astype(BF16).astype(F32)
+    low = dg_old - high - mid
+    mail32[:, 15] = jnp.zeros((nz, ln), F32)
+    for at, part in enumerate((high, mid, low)):
+        mail32[:, 9 + 2 * at] = part[:, :ln]
+        mail32[:, 10 + 2 * at] = part[:, ln:]
+
+    def xy_sum(o, total):
+        xy_copy(o).wait_recv()
+        return total + from_xy[o - 1].astype(F32)
+
+    summed = lax.fori_loop(1, nx * ny, xy_sum, grad[c, y, x] + from_core[y, x].astype(F32))
     for tap in range(9):
-        mail[:, tap] = summed[:, tap * ln : (tap + 1) * ln]
+        mail32[:, tap] = summed[:, tap * ln : (tap + 1) * ln]
+    mail[...] = mail32[...].astype(BF16)
 
     give_back(4, mail, from_z)
     arrived(4, from_z)
-    both = [jnp.zeros((11, ln), F32), jnp.zeros((11, ln), F32)]
+    both = [jnp.zeros((16, ln), F32), jnp.zeros((16, ln), F32)]
     for k in range(nz):
-        both[k % 2] = both[k % 2] + from_z[k]
+        both[k % 2] = both[k % 2] + from_z[k].astype(F32)
     share[:9] = both[0][:9]
     share[9:18] = both[1][:9]
-    share[18:20] = both[0][9:] + both[1][9:]
+    rest = both[0] + both[1]
+    share[18:20] = rest[9:11] + (rest[11:13] + rest[13:15])
 
     def share_copy(o):
         return pltpu.make_async_remote_copy(
@@ -399,16 +425,12 @@
 
     for o in range(1, 2 * ny):
         share_copy(o).start()
-    shares[spot] = share[...]
+    own = pltpu.make_async_copy(share, shares.at[spot], put_sem.at[1])
+    own.start()
     for o in range(1, 2 * ny):
         share_copy(o).wait_recv()
-    for j in range(ny):
-        din_ref[j] = (shares[2 * j, :9] + shares[2 * j + 1, :9]) * wscale
-        dout_ref[j] = (shares[2 * j, 9:18] + shares[2 * j + 1, 9:18]) * wscale
-    total = shares[0, 18:20]
-    for s in range(1, 2 * ny):
-        total += shares[s, 18:20]
-    dg_ref[...] = total * dscale
+    own.wait()
+    put_dinp.wait()
 
     sent(0, dec_in)
     sent(1, send_c)
@@ -421,12 +443,34 @@
         pl.when(to < x)(carry_copy(carry_a, carries_a, 0, to).wait_send)
         pl.when(to > x)(carry_copy(carry_s, carries_s, 1, to).wait_send)
     core_copy().wait_send()
-    for o in range(1, ny):
-        y_copy(o).wait_send()
-    for o in range(1, nx):
-        x_copy(o).wait_send()
+
+    @pl.loop(1, nx * ny)
+    def _(o):
+        xy_copy(o).wait_send()
+
     for o in range(1, 2 * ny):
         share_copy(o).wait_send()
+
+
+def finish(ny, ln, wscale, dscale, dinp_hbm, shares_hbm, out_hbm, din_ref, dout_ref, dg_ref, shares, tile, sem):
+    fetch = pltpu.make_async_copy(shares_hbm, shares, sem.at[0])
+    come = pltpu.make_async_copy(dinp_hbm, tile, sem.at[1])
+    go = pltpu.make_async_copy(tile, out_hbm, sem.at[2])
+    come.start()
+    fetch.start()
+    come.wait()
+    go.start()
+    fetch.wait()
+    for j in range(ny):
+        both = shares[2 * j] + shares[2 * j + 1]
+        din_ref[:, j] = both[:9] * wscale
+        dout_ref[:, j] = both[9:18] * wscale
+    total = shares[0, 18:20]
+    for s in range(1, 2 * ny):
+        total += shares[s, 18:20]
+    dg_ref[:, :ln] = total[:1] * dscale
+    dg_ref[:, ln:] = total[1:] * dscale
+    go.wait()
 
 
 def body(nx, inputs, cotangent, w_in, w_out, decay, skip):
@@ -441,6 +485,13 @@
     vmem = pltpu.VMEM
     dma = pltpu.SemaphoreType.DMA
     scratch = [
+        vmem((rows, wide, ln), BF16),
+        vmem((rows, wide, ln), BF16),
+        vmem((9, ln, states), BF16),
+        vmem((9, states, ln), BF16),
+        vmem((1, states), F32),
+        vmem((1, ln), F32),
+        dma((6,)),
         vmem((block, ln), F32),
         vmem((nz, cells, ln), BF16),
         vmem((nz, cells, ln), BF16),
@@ -466,18 +517,17 @@
         vmem((nx, 2, cells + 8, ln), F32),
         vmem((2, cells, ln), F32),
         vmem((2, nz, ln), F32),
-        vmem((2, ny, nx * nz, 9 * ln), F32),
-        vmem((ny, nx * nz, 9 * ln), BF16),
-        vmem((ny, nx * nz, 9 * ln), BF16),
-        vmem((ny, nx * nz, 9 * ln), BF16),
-        vmem((ny - 1, nx * nz, 9 * ln), BF16),
-        vmem((nx, nz, 9 * ln), F32),
-        vmem((nx, nz, 9 * ln), BF16),
-        vmem((nx - 1, nz, 9 * ln), BF16),
-        vmem((nz, 11, ln), F32),
-        vmem((nz, 11, ln), F32),
+        vmem((2, ny, nx, nz, 9 * ln), F32),
+        vmem((ny, nx, nz, 9 * ln), BF16),
+        vmem((ny, nx, nz, 9 * ln), BF16),
+        vmem((ny, nx, nz, 9 * ln), BF16),
+        vmem((nx * ny - 1, nz, 9 * ln), BF16),
+        vmem((nz, 16, ln), F32),
+        vmem((nz, 16, ln), BF16),
+        vmem((nz, 16, ln), BF16),
         vmem((20, ln), F32),
-        vmem((2 * ny, 20, ln), F32),
+        vmem((rows, wide, ln), BF16),
+        dma((2,)),
         dma((5,)),
         dma((5,)),
         dma((3, 8)),
@@ -485,26 +535,20 @@
         dma((2, nx)),
         dma((2, nx)),
         dma((2,)),
-        dma((ny - 1,)),
-        dma((ny - 1,)),
-        dma((nx - 1,)),
-        dma((nx - 1,)),
+        dma((nx * ny - 1,)),
+        dma((nx * ny - 1,)),
         dma((2 * ny - 1,)),
         dma((2 * ny - 1,)),
     ]
-    d_inputs, d_in, d_out, d_decay = pl.pallas_call(
-        functools.partial(kernel, nx, nz, ny, rows, ln, wscale, dscale),
-        out_shape=(
-            jax.ShapeDtypeStruct((rows, wide, ln), BF16),
-            jax.ShapeDtypeStruct((ny, 9, ln), F32),
-            jax.ShapeDtypeStruct((ny, 9, ln), F32),
-            jax.ShapeDtypeStruct((2, ln), F32),
-        ),
-        in_specs=[pl.BlockSpec(memory_space=pltpu.VMEM)] * 6,
-        out_specs=tuple([pl.BlockSpec(memory_space=pltpu.VMEM)] * 4),
+    tile = jax.ShapeDtypeStruct((rows, wide, ln), BF16)
+    d_inputs, shares = pl.pallas_call(
+        functools.partial(kernel, nx, nz, ny, rows, ln),
+        out_shape=(tile, jax.ShapeDtypeStruct((2 * ny, 20, ln), F32)),
+        in_specs=[pl.BlockSpec(memory_space=pltpu.HBM)] * 6,
+        out_specs=(pl.BlockSpec(memory_space=pltpu.HBM), pl.BlockSpec(memory_space=pltpu.HBM)),
         scratch_shapes=scratch,
         compiler_params=pltpu.CompilerParams(
-            collective_id=0, has_side_effects=True, vmem_limit_bytes=48 * 1024 * 1024
+            collective_id=0, has_side_effects=True, vmem_limit_bytes=63 * 1024 * 1024
         ),
         cost_estimate=pl.CostEstimate(
             flops=5 * 2 * block * 9 * ln * states, bytes_accessed=4 * 1024 * 1024, transcendentals=0
@@ -517,12 +561,25 @@
         decay,
         skip.reshape(1, ln),
     )
-    return (
-        d_inputs[None],
-        d_in.reshape(ny, 3, 3, ln),
-        d_out.reshape(ny, 3, 3, ln),
-        d_decay.reshape(1, states),
-    )
+    whole = pl.BlockSpec(memory_space=pltpu.VMEM)
+    d_inputs, d_in, d_out, d_decay = pl.pallas_call(
+        functools.partial(finish, ny, ln, wscale, dscale),
+        out_shape=(
+            tile,
+            jax.ShapeDtypeStruct((9, ny, ln), F32),
+            jax.ShapeDtypeStruct((9, ny, ln), F32),
+            jax.ShapeDtypeStruct((1, states), F32),
+        ),
+        in_specs=[pl.BlockSpec(memory_space=pltpu.HBM)] * 2,
+        out_specs=(pl.BlockSpec(memory_space=pltpu.HBM), whole, whole, whole),
+        scratch_shapes=[vmem((2 * ny, 20, ln), F32), vmem((rows, wide, ln), BF16), dma((3,))],
+        compiler_params=pltpu.CompilerParams(vmem_limit_bytes=63 * 1024 * 1024),
+    )(d_inputs, shares)
+
+    def by_channel(grad):
+        return jnp.transpose(grad.reshape(3, 3, ny, ln), (2, 0, 1, 3))
+
+    return (d_inputs[None], by_channel(d_in), by_channel(d_out), d_decay)
 
 
 def solution(mesh, nx=X_CHIPS):

time: 80.8 us -> 74.8 us (0.926)
  local copies, waits for them, and re-layouts: 7.05 us -> 0 us
  Pallas kernels: 72.9 us -> 74 us
    unnamed x14 -> x0, local copies, waits for them, and re-layouts: 5.82 us -> none
    pallas_call x2 -> x0, local copies, waits for them, and re-layouts: 1.23 us -> none  [body(): pl.pallas_call(functools.partial(kernel, nx, nz, ny, rows, ln, wscale, ds...]
    pallas_call x1 -> x2, Pallas kernels: 72.9 us -> 74 us  [the longest x1 71.8 us: body(): pl.pallas_call(functools.partial(kernel, nx, nz, ny, rows, ln), out_shape...]
where the time goes in v2:
time: 74.8 us; the launch traced here: 74.6 us
  Pallas kernels  74 us (99%)
    pallas_call x1, Pallas kernels, body(): pl.pallas_call(functools.partial(kernel, nx, nz, ny, rows, ln), out_shape...  71.8 us
    pallas_call x1, Pallas kernels, body(): pl.pallas_call(functools.partial(finish, ny, ln, wscale, dscale), out_sha...  2.2 us

profile of v2, /device:TPU:1, one launch (start us, length us, event | category | flops | bytes accessed | tf_op | source)
XLA Modules:
  0.0 74.6 jit_solution(7338000990602356060)
XLA Ops:
  0.6 71.8 %shard_map.93 = (bf16[16,32,128]{2,1,0:T(8,128)(2,1)}, f32[8,20,128]{2,1,0:T(8,128)}) custom-call(bf16[16,32,128]{2,1,0:T(8,128)(2,1)} %bitcast.14, bf16[16,32,128]{2,1,0:T(8,128)(2,1)} %bitcast.15, bf16[9,128,256]{2,1,0:T(8,128)(2,1)} %bitcast.12, bf16[9,256,128]{2,1,0:T(8,128)(2,1)} %bitcast.13, f32[1,256]{1,0:T(1,128)} %dec_hbm.1, f32[1,128]{1,0:T(1,128)} %bitcast.19), custom_call_target="tpu_custom_call" | custom-call | flops 1509949440 | bytes 4194304 | tf_op jit(solution)/shard_map/pallas_call | solution.py:544
  72.4 2.2 %shard_map.94 = (bf16[16,32,128]{2,1,0:T(8,128)(2,1)}, f32[9,4,128]{2,1,0:T(4,128)}, f32[9,4,128]{2,1,0:T(4,128)}, f32[1,256]{1,0:T(1,128)}) custom-call(bf16[16,32,128]{2,1,0:T(8,128)(2,1)} %get-tuple-element.10.dinp_hbm, f32[8,20,128]{2,1,0:T(8,128)} %get-tuple-element.11.shares_hbm), custom_call_target="tpu_custom_call" | custom-call | tf_op jit(solution)/shard_map/pallas_call | solution.py:565

commit v3 on v2

--- a/solution.py
+++ b/solution.py
@@ -124,27 +124,34 @@
                     pl.ds(2 * k + col, rows, stride=wide)
                 ].astype(BF16)
 
+    def chip(i):
+        odd = i % 2
+        return (z + nz // 2 + (1 - odd) * (i // 2) - odd * ((i + 1) // 2) + nz) % nz
+
     def scatter(at, source, target):
         @pl.loop(0, nz)
-        def _(o):
-            k = (z + o) % nz
-            to = c * nz + k
-
-            @pl.when(to == q)
-            def _():
-                pltpu.make_async_copy(source(k), target.at[z], p1_recv.at[at]).start()
-
-            @pl.when(to != q)
-            def _():
-                pltpu.make_async_remote_copy(
-                    source(k), target.at[z], p1_send.at[at], p1_recv.at[at],
-                    device_id=(x * nz + to // 2, y, to % 2), device_id_type=MESH,
-                ).start()
+        def _(i):
+            to = chip(i)
+            for core in range(2):
+                k = 2 * to + core - c * nz
+                wanted = (k >= 0) & (k < nz)
+                own = (to == z) & (c == core)
+
+                @pl.when(wanted & own)
+                def _():
+                    pltpu.make_async_copy(source(k), target.at[z], p1_recv.at[at]).start()
+
+                @pl.when(wanted & jnp.logical_not(own))
+                def _():
+                    pltpu.make_async_remote_copy(
+                        source(k), target.at[z], p1_send.at[at], p1_recv.at[at],
+                        device_id=(x * nz + to, y, core), device_id_type=MESH,
+                    ).start()
 
     def give_back(at, source, target):
         @pl.loop(0, nz)
-        def _(o):
-            t = (z + o) % nz
+        def _(i):
+            t = chip(i)
             own = paired & (t == z)
 
             @pl.when(own)
@@ -261,6 +268,9 @@
     arrived(1, recv_c)
     unpack(recv_c, pad_c)
     halo(0, pad_c, "send")
+    arrived(2, recv_i)
+    unpack(recv_i, pad_i)
+    halo(1, pad_i, "send")
     halo(0, pad_c, "arrive")
     lay_out(pad_c, cols_c, True)
     value = dot(cols_c[...], w_exc[...], ((1,), (0,)))
@@ -282,22 +292,6 @@
     for to in range(nx):
         pl.when(to < x)(carry_copy(carry_a, carries_a, 0, to).start)
 
-    arrived(2, recv_i)
-    unpack(recv_i, pad_i)
-    halo(1, pad_i, "send")
-
-    fold(carries_a, 0, range(nx - 1, -1, -1), lambda source: source > x)
-    for h in range(2):
-        def adjoint_final(i, b):
-            t = nz - 1 - i
-            level = exc[h, frame(t)] + b
-            exc[h, frame(t)] = level
-            return decp[h, pl.ds(t, 1)] * level
-
-        lax.fori_loop(0, nz, adjoint_final, entry[h])
-    adjoint_b = jnp.concatenate([exc[0], exc[1]], axis=1).astype(BF16)
-    pad_a[1:3, 1 : 1 + rows] = adjoint_b.reshape(2, rows, nz, states)
-    halo(2, pad_a, "send")
 
     halo(1, pad_i, "arrive")
     lay_out(pad_i, cols_i, False)
@@ -313,6 +307,19 @@
     for to in range(nx):
         pl.when(to > x)(carry_copy(carry_s, carries_s, 1, to).start)
 
+    fold(carries_a, 0, range(nx - 1, -1, -1), lambda source: source > x)
+    for h in range(2):
+        def adjoint_final(i, b):
+            t = nz - 1 - i
+            level = exc[h, frame(t)] + b
+            exc[h, frame(t)] = level
+            return decp[h, pl.ds(t, 1)] * level
+
+        lax.fori_loop(0, nz, adjoint_final, entry[h])
+    adjoint_b = jnp.concatenate([exc[0], exc[1]], axis=1).astype(BF16)
+    pad_a[1:3, 1 : 1 + rows] = adjoint_b.reshape(2, rows, nz, states)
+    halo(2, pad_a, "send")
+
     def core_copy():
         return pltpu.make_async_remote_copy(
             grad_b, from_core, core_sem.at[0], core_sem.at[1],
@@ -342,8 +349,6 @@
     def _():
         grad_b[...] = grad[0].astype(BF16)
         core_copy().start()
-
-    pl.when(c == 0)(begin)
 
     fold(carries_s, 1, range(nx), lambda source: source < x)
     for h in range(2):
@@ -362,7 +367,7 @@
         grad_b[...] = grad[1].astype(BF16)
         core_copy().start()
 
-    pl.when(c == 1)(begin)
+    begin()
 
     halo(2, pad_a, "arrive")
     total = skip_ref[...] * pad_c[1:3, 1 : 1 + rows].reshape(block, ln).astype(F32)
@@ -376,16 +381,6 @@
         send_d[t] = t32[frame(t)].astype(BF16)
 
     give_back(3, send_d, recv_d)
-
-    arrived(3, recv_d)
-    t32[...] = recv_d[...].astype(F32).reshape(block, ln)
-
-    @pl.loop(0, rows)
-    def _(r):
-        dinp_ref[r] = t32[pl.ds(r, wide, stride=rows)].astype(BF16)
-
-    put_dinp = pltpu.make_async_copy(dinp_ref, dinp_hbm, put_sem.at[0])
-    put_dinp.start()
 
     dg_old = exact_dot(
         jnp.concatenate([dg_part[0], dg_part[1]], axis=1), perm, ((1,), (1,))
@@ -408,6 +403,17 @@
     mail[...] = mail32[...].astype(BF16)
 
     give_back(4, mail, from_z)
+
+    arrived(3, recv_d)
+    t32[...] = recv_d[...].astype(F32).reshape(block, ln)
+
+    @pl.loop(0, rows)
+    def _(r):
+        dinp_ref[r] = t32[pl.ds(r, wide, stride=rows)].astype(BF16)
+
+    put_dinp = pltpu.make_async_copy(dinp_ref, dinp_hbm, put_sem.at[0])
+    put_dinp.start()
+
     arrived(4, from_z)
     both = [jnp.zeros((16, ln), F32), jnp.zeros((16, ln), F32)]
     for k in range(nz):

time: 74.8 us -> 68.9 us (0.921)
  Pallas kernels: 74 us -> 68.1 us
    pallas_call x1, Pallas kernels: 71.8 us -> 65.9 us  [body(): pl.pallas_call(functools.partial(kernel, nx, nz, ny, rows, ln), out_shape...]
where the time goes in v3:
time: 68.9 us; the launch traced here: 68.7 us
  Pallas kernels  68.1 us (99%)
    pallas_call x1, Pallas kernels, body(): pl.pallas_call(functools.partial(kernel, nx, nz, ny, rows, ln), out_shape...  65.9 us
    pallas_call x1, Pallas kernels, body(): pl.pallas_call(functools.partial(finish, ny, ln, wscale, dscale), out_sha...  2.2 us

profile of v3, /device:TPU:1, one launch (start us, length us, event | category | flops | bytes accessed | tf_op | source)
XLA Modules:
  0.0 68.7 jit_solution(362572531418281747)
XLA Ops:
  0.6 65.9 %shard_map.93 = (bf16[16,32,128]{2,1,0:T(8,128)(2,1)}, f32[8,20,128]{2,1,0:T(8,128)}) custom-call(bf16[16,32,128]{2,1,0:T(8,128)(2,1)} %bitcast.14, bf16[16,32,128]{2,1,0:T(8,128)(2,1)} %bitcast.15, bf16[9,128,256]{2,1,0:T(8,128)(2,1)} %bitcast.12, bf16[9,256,128]{2,1,0:T(8,128)(2,1)} %bitcast.13, f32[1,256]{1,0:T(1,128)} %dec_hbm.1, f32[1,128]{1,0:T(1,128)} %bitcast.19), custom_call_target="tpu_custom_call" | custom-call | flops 1509949440 | bytes 4194304 | tf_op jit(solution)/shard_map/pallas_call | solution.py:550
  66.5 2.2 %shard_map.94 = (bf16[16,32,128]{2,1,0:T(8,128)(2,1)}, f32[9,4,128]{2,1,0:T(4,128)}, f32[9,4,128]{2,1,0:T(4,128)}, f32[1,256]{1,0:T(1,128)}) custom-call(bf16[16,32,128]{2,1,0:T(8,128)(2,1)} %get-tuple-element.10.dinp_hbm, f32[8,20,128]{2,1,0:T(8,128)} %get-tuple-element.11.shares_hbm), custom_call_target="tpu_custom_call" | custom-call | tf_op jit(solution)/shard_map/pallas_call | solution.py:571

commit v4 on v3

--- a/solution.py
+++ b/solution.py
@@ -40,7 +40,7 @@
     grad, grad_b, from_core, part_b, from_xy,
     mail32, mail, from_z, share, dinp_ref, put_sem,
     p1_send, p1_recv, halo_send, halo_recv, car_send, car_recv,
-    core_sem, xy_send, xy_recv, ag_send, ag_recv,
+    core_send, core_recv, xy_send, xy_recv, ag_send, ag_recv,
 ):
     cells = 2 * rows
     wide = 2 * nz
@@ -73,6 +73,10 @@
         to = (spot + o) % (2 * ny)
         return (tm, to // 2, to % 2)
 
+    def chip(i):
+        odd = i % 2
+        return (z + nz // 2 + (1 - odd) * (i // 2) - odd * ((i + 1) // 2) + nz) % nz
+
     fetches = [
         pltpu.make_async_copy(source, target, fetch_sem.at[at])
         for at, (source, target) in enumerate([
@@ -89,7 +93,9 @@
         pl.semaphore_signal(barrier, inc=1, device_id=device, device_id_type=MESH)
 
     @pl.loop(0, nz)
-    def _(t):
+    def _(i):
+        t = chip(i)
+
         @pl.when(jnp.logical_not(paired & (t == z)))
         def _():
             greet((x * nz + t, y, home))
@@ -123,10 +129,6 @@
                 out[k, col * rows : (col + 1) * rows] = t32[
                     pl.ds(2 * k + col, rows, stride=wide)
                 ].astype(BF16)
-
-    def chip(i):
-        odd = i % 2
-        return (z + nz // 2 + (1 - odd) * (i // 2) - odd * ((i + 1) // 2) + nz) % nz
 
     def scatter(at, source, target):
         @pl.loop(0, nz)
@@ -292,7 +294,6 @@
     for to in range(nx):
         pl.when(to < x)(carry_copy(carry_a, carries_a, 0, to).start)
 
-
     halo(1, pad_i, "arrive")
     lay_out(pad_i, cols_i, False)
     value = dot(cols_i[...], w_src[...], ((1,), (0,)))
@@ -320,15 +321,14 @@
     pad_a[1:3, 1 : 1 + rows] = adjoint_b.reshape(2, rows, nz, states)
     halo(2, pad_a, "send")
 
-    def core_copy():
+    half = ny // 2
+
+    def core_copy(h):
+        part = pl.ds(h * half, half)
         return pltpu.make_async_remote_copy(
-            grad_b, from_core, core_sem.at[0], core_sem.at[1],
+            grad_b.at[part], from_core.at[part], core_send.at[h], core_recv.at[h],
             device_id=(tm, y, 1 - c), device_id_type=MESH,
         )
-
-    grad[0] = dot(
-        pad_a[1:3, 1 : 1 + rows].reshape(block, states), cols_i[...], ((0,), (0,))
-    ).reshape(grad.shape[1:])
 
     def xy_copy(o):
         to = (flat + o) % (nx * ny)
@@ -337,18 +337,29 @@
             device_id=flat_id(o), device_id_type=MESH,
         )
 
+    def gradient(which, h, levels, cols):
+        part = slice(h * half, (h + 1) * half)
+        value = dot(levels[h].astype(BF16), cols[...], ((0,), (0,)))
+        grad[which, part] = value.reshape(half, nx, nz, 9 * ln)
+
+        @pl.when(c != which)
+        def _():
+            grad_b[part] = grad[which, part].astype(BF16)
+            core_copy(h).start()
+
     def begin():
-        core_copy().wait_recv()
-        part_b[...] = (grad[c] + from_core[...].astype(F32)).astype(BF16)
-
-        @pl.loop(1, nx * ny)
-        def _(o):
-            xy_copy(o).start()
-
-    @pl.when(c == 1)
-    def _():
-        grad_b[...] = grad[0].astype(BF16)
-        core_copy().start()
+        for h in range(2):
+            core_copy(h).wait_recv()
+            part = slice(h * half, (h + 1) * half)
+            part_b[part] = (grad[c, part] + from_core[part].astype(F32)).astype(BF16)
+
+            @pl.loop(1, nx * ny)
+            def _(o):
+                pl.when(((flat + o) % ny) // half == h)(lambda: xy_copy(o).start())
+
+    for h in range(2):
+        gradient(0, h, exc, cols_i)
+    pl.when(c == 0)(begin)
 
     fold(carries_s, 1, range(nx), lambda source: source < x)
     for h in range(2):
@@ -359,15 +370,8 @@
             return now
 
         lax.fori_loop(0, nz, state_final, entry[h])
-    state_b = jnp.concatenate([src[0], src[1]], axis=1).astype(BF16)
-    grad[1] = dot(state_b, cols_c[...], ((0,), (0,))).reshape(grad.shape[1:])
-
-    @pl.when(c == 0)
-    def _():
-        grad_b[...] = grad[1].astype(BF16)
-        core_copy().start()
-
-    begin()
+        gradient(1, h, src, cols_c)
+    pl.when(c == 1)(begin)
 
     halo(2, pad_a, "arrive")
     total = skip_ref[...] * pad_c[1:3, 1 : 1 + rows].reshape(block, ln).astype(F32)
@@ -448,7 +452,8 @@
     for to in range(nx):
         pl.when(to < x)(carry_copy(carry_a, carries_a, 0, to).wait_send)
         pl.when(to > x)(carry_copy(carry_s, carries_s, 1, to).wait_send)
-    core_copy().wait_send()
+    for h in range(2):
+        core_copy(h).wait_send()
 
     @pl.loop(1, nx * ny)
     def _(o):
@@ -541,6 +546,7 @@
         dma((2, nx)),
         dma((2, nx)),
         dma((2,)),
+        dma((2,)),
         dma((nx * ny - 1,)),
         dma((nx * ny - 1,)),
         dma((2 * ny - 1,)),

time: 68.9 us -> 67.3 us (0.977)
  Pallas kernels: 68.1 us -> 66.5 us
    pallas_call x1, Pallas kernels: 65.9 us -> 64.3 us  [body(): pl.pallas_call(functools.partial(kernel, nx, nz, ny, rows, ln), out_shape...]
where the time goes in v4:
time: 67.3 us; the launch traced here: 67.2 us
  Pallas kernels  66.5 us (99%)
    pallas_call x1, Pallas kernels, body(): pl.pallas_call(functools.partial(kernel, nx, nz, ny, rows, ln), out_shape...  64.3 us
    pallas_call x1, Pallas kernels, body(): pl.pallas_call(functools.partial(finish, ny, ln, wscale, dscale), out_sha...  2.2 us

profile of v4, /device:TPU:1, one launch (start us, length us, event | category | flops | bytes accessed | tf_op | source)
XLA Modules:
  0.0 67.2 jit_solution(2373965819674150536)
XLA Ops:
  0.6 64.3 %shard_map.93 = (bf16[16,32,128]{2,1,0:T(8,128)(2,1)}, f32[8,20,128]{2,1,0:T(8,128)}) custom-call(bf16[16,32,128]{2,1,0:T(8,128)(2,1)} %bitcast.14, bf16[16,32,128]{2,1,0:T(8,128)(2,1)} %bitcast.15, bf16[9,128,256]{2,1,0:T(8,128)(2,1)} %bitcast.12, bf16[9,256,128]{2,1,0:T(8,128)(2,1)} %bitcast.13, f32[1,256]{1,0:T(1,128)} %dec_hbm.1, f32[1,128]{1,0:T(1,128)} %bitcast.19), custom_call_target="tpu_custom_call" | custom-call | flops 1509949440 | bytes 4194304 | tf_op jit(solution)/shard_map/pallas_call | solution.py:556
  65.0 2.2 %shard_map.94 = (bf16[16,32,128]{2,1,0:T(8,128)(2,1)}, f32[9,4,128]{2,1,0:T(4,128)}, f32[9,4,128]{2,1,0:T(4,128)}, f32[1,256]{1,0:T(1,128)}) custom-call(bf16[16,32,128]{2,1,0:T(8,128)(2,1)} %get-tuple-element.10.dinp_hbm, f32[8,20,128]{2,1,0:T(8,128)} %get-tuple-element.11.shares_hbm), custom_call_target="tpu_custom_call" | custom-call | tf_op jit(solution)/shard_map/pallas_call | solution.py:577

commit v5 on v4

--- a/solution.py
+++ b/solution.py
@@ -13,7 +13,12 @@
 BF16 = jnp.bfloat16
 X_CHIPS = 4
 TAPS = [(di, dj) for di in range(3) for dj in range(3)]
-SIDES = [(dr, dc) for dr in (-1, 0, 1) for dc in (-1, 0, 1) if dr or dc]
+SIDES = [(0, -1), (0, 1), (-1, -1), (1, 1), (-1, 1), (1, -1), (-1, 0), (1, 0)]
+
+
+def far(i, n):
+    odd = i % 2
+    return n // 2 + (1 - odd) * (i // 2) - odd * ((i + 1) // 2)
 
 
 def dot(a, b, dims):
@@ -56,7 +61,6 @@
     place = q % nz
     paired = home == c
     spot = 2 * y + c
-    flat = x * ny + y
 
     def here(dr, dc):
         return (y + dr >= 0) & (y + dr < ny) & (q + dc >= 0) & (q + dc < wide)
@@ -65,17 +69,19 @@
         to = q + dc
         return (x * nz + to // 2, y + dr, to % 2)
 
-    def flat_id(o):
-        to = (flat + o) % (nx * ny)
-        return ((to // ny) * nz + z, to % ny, c)
+    def flat_to(i):
+        return (x + far(i // ny, nx)) % nx, (y + far(i % ny, ny)) % ny
+
+    def flat_id(i):
+        to_x, to_y = flat_to(i)
+        return (to_x * nz + z, to_y, c)
 
     def spot_id(o):
         to = (spot + o) % (2 * ny)
         return (tm, to // 2, to % 2)
 
     def chip(i):
-        odd = i % 2
-        return (z + nz // 2 + (1 - odd) * (i // 2) - odd * ((i + 1) // 2) + nz) % nz
+        return (z + far(i, nz)) % nz
 
     fetches = [
         pltpu.make_async_copy(source, target, fetch_sem.at[at])
@@ -100,9 +106,11 @@
         def _():
             greet((x * nz + t, y, home))
 
-    @pl.loop(1, nx * ny)
-    def _(o):
-        greet(flat_id(o))
+    others = nx * ny - 1
+
+    @pl.loop(0, others)
+    def _(i):
+        greet(flat_id(i))
 
     for o in range(1, 2 * ny, 2):
         greet((tm, (y + o // 2) % ny, 1 - c))
@@ -188,9 +196,9 @@
     scatter(1, lambda k: send_c.at[k], recv_c)
     fetches[1].wait()
     pack(in_ref, send_i)
+    scatter(2, lambda k: send_i.at[k], recv_i)
     fetches[2].wait()
     scatter(0, lambda k: dec_ref, dec_in)
-    scatter(2, lambda k: send_i.at[k], recv_i)
     fetches[3].wait()
     fetches[4].wait()
     fetches[5].wait()
@@ -205,11 +213,6 @@
         w_src[at] = dot(win_ref[tap], perm, ((1,), (0,))).astype(BF16)
         w_exc[at] = dot(wout_ref[tap], perm, ((0,), (0,))).astype(BF16)
         w_back[tap] = dot(perm, win_ref[tap], ((0,), (1,))).astype(BF16)
-
-    arrived(0, dec_in)
-    rates = exact_dot(dec_in[...].reshape(nz, states), perm, ((1,), (0,)))
-    decp[0] = rates[:, :ln]
-    decp[1] = rates[:, ln:]
 
     def unpack(recv, pad):
         t32[...] = recv[...].astype(F32).reshape(block, ln)
@@ -273,6 +276,10 @@
     arrived(2, recv_i)
     unpack(recv_i, pad_i)
     halo(1, pad_i, "send")
+    arrived(0, dec_in)
+    rates = exact_dot(dec_in[...].reshape(nz, states), perm, ((1,), (0,)))
+    decp[0] = rates[:, :ln]
+    decp[1] = rates[:, ln:]
     halo(0, pad_c, "arrive")
     lay_out(pad_c, cols_c, True)
     value = dot(cols_c[...], w_exc[...], ((1,), (0,)))
@@ -330,11 +337,11 @@
             device_id=(tm, y, 1 - c), device_id_type=MESH,
         )
 
-    def xy_copy(o):
-        to = (flat + o) % (nx * ny)
+    def xy_copy(i):
+        to_x, to_y = flat_to(i)
         return pltpu.make_async_remote_copy(
-            part_b.at[to % ny, to // ny], from_xy.at[o - 1], xy_send.at[o - 1], xy_recv.at[o - 1],
-            device_id=flat_id(o), device_id_type=MESH,
+            part_b.at[to_y, to_x], from_xy.at[i], xy_send.at[i], xy_recv.at[i],
+            device_id=flat_id(i), device_id_type=MESH,
         )
 
     def gradient(which, h, levels, cols):
@@ -353,9 +360,9 @@
             part = slice(h * half, (h + 1) * half)
             part_b[part] = (grad[c, part] + from_core[part].astype(F32)).astype(BF16)
 
-            @pl.loop(1, nx * ny)
-            def _(o):
-                pl.when(((flat + o) % ny) // half == h)(lambda: xy_copy(o).start())
+            @pl.loop(0, others)
+            def _(i):
+                pl.when(flat_to(i)[1] // half == h)(lambda: xy_copy(i).start())
 
     for h in range(2):
         gradient(0, h, exc, cols_i)
@@ -397,11 +404,11 @@
         mail32[:, 9 + 2 * at] = part[:, :ln]
         mail32[:, 10 + 2 * at] = part[:, ln:]
 
-    def xy_sum(o, total):
-        xy_copy(o).wait_recv()
-        return total + from_xy[o - 1].astype(F32)
-
-    summed = lax.fori_loop(1, nx * ny, xy_sum, grad[c, y, x] + from_core[y, x].astype(F32))
+    def xy_sum(i, total):
+        xy_copy(i).wait_recv()
+        return total + from_xy[i].astype(F32)
+
+    summed = lax.fori_loop(0, others, xy_sum, grad[c, y, x] + from_core[y, x].astype(F32))
     for tap in range(9):
         mail32[:, tap] = summed[:, tap * ln : (tap + 1) * ln]
     mail[...] = mail32[...].astype(BF16)
@@ -433,7 +440,7 @@
             device_id=spot_id(o), device_id_type=MESH,
         )
 
-    for o in range(1, 2 * ny):
+    for o in sorted(range(1, 2 * ny), key=lambda o: -min(o, 2 * ny - o)):
         share_copy(o).start()
     own = pltpu.make_async_copy(share, shares.at[spot], put_sem.at[1])
     own.start()
@@ -455,9 +462,9 @@
     for h in range(2):
         core_copy(h).wait_send()
 
-    @pl.loop(1, nx * ny)
-    def _(o):
-        xy_copy(o).wait_send()
+    @pl.loop(0, others)
+    def _(i):
+        xy_copy(i).wait_send()
 
     for o in range(1, 2 * ny):
         share_copy(o).wait_send()

time: 67.3 us -> 67.9 us (level)
  no operation moved by 1% of the time
where the time goes in v5:
time: 67.9 us; the launch traced here: 67.6 us
  Pallas kernels  66.9 us (99%)
    pallas_call x1, Pallas kernels, body(): pl.pallas_call(functools.partial(kernel, nx, nz, ny, rows, ln), out_shape...  64.7 us
    pallas_call x1, Pallas kernels, body(): pl.pallas_call(functools.partial(finish, ny, ln, wscale, dscale), out_sha...  2.2 us

profile of v5, /device:TPU:1, one launch (start us, length us, event | category | flops | bytes accessed | tf_op | source)
XLA Modules:
  0.0 67.6 jit_solution(14965574334980568424)
XLA Ops:
  0.6 64.7 %shard_map.93 = (bf16[16,32,128]{2,1,0:T(8,128)(2,1)}, f32[8,20,128]{2,1,0:T(8,128)}) custom-call(bf16[16,32,128]{2,1,0:T(8,128)(2,1)} %bitcast.14, bf16[16,32,128]{2,1,0:T(8,128)(2,1)} %bitcast.15, bf16[9,128,256]{2,1,0:T(8,128)(2,1)} %bitcast.12, bf16[9,256,128]{2,1,0:T(8,128)(2,1)} %bitcast.13, f32[1,256]{1,0:T(1,128)} %dec_hbm.1, f32[1,128]{1,0:T(1,128)} %bitcast.19), custom_call_target="tpu_custom_call" | custom-call | flops 1509949440 | bytes 4194304 | tf_op jit(solution)/shard_map/pallas_call | solution.py:563
  65.4 2.2 %shard_map.94 = (bf16[16,32,128]{2,1,0:T(8,128)(2,1)}, f32[9,4,128]{2,1,0:T(4,128)}, f32[9,4,128]{2,1,0:T(4,128)}, f32[1,256]{1,0:T(1,128)}) custom-call(bf16[16,32,128]{2,1,0:T(8,128)(2,1)} %get-tuple-element.10.dinp_hbm, f32[8,20,128]{2,1,0:T(8,128)} %get-tuple-element.11.shares_hbm), custom_call_target="tpu_custom_call" | custom-call | tf_op jit(solution)/shard_map/pallas_call | solution.py:584

commit v6 on v5

--- a/solution.py
+++ b/solution.py
@@ -264,9 +264,12 @@
             def _():
                 carry_from(recv, which, source).wait()
                 for h in range(2):
-                    entry[h] = (
-                        recv[source, h, :cells] + recv[source, h, cells : cells + 1] * entry[h]
+                    held = recv[source, h].astype(F32)
+                    factor = (
+                        held[cells : cells + 1] + held[cells + 1 : cells + 2]
+                        + held[cells + 2 : cells + 3]
                     )
+                    entry[h] = held[:cells] + factor * entry[h]
 
     frame = lambda t: pl.ds(t, cells, stride=nz)
 
@@ -296,8 +299,14 @@
         b, factor = lax.fori_loop(
             0, nz, adjoint_step, (jnp.zeros((cells, ln), F32), jnp.ones((1, ln), F32))
         )
-        carry_a[h, :cells] = b
-        carry_a[h, cells:] = jnp.broadcast_to(factor, (8, ln))
+        high = factor.astype(BF16).astype(F32)
+        mid = (factor - high).astype(BF16).astype(F32)
+        row = lax.broadcasted_iota(jnp.int32, (16, ln), 0)
+        parts = jnp.where(
+            row == 0, high, jnp.where(row == 1, mid, jnp.where(row == 2, factor - high - mid, 0.0))
+        )
+        carry_a[h, :cells] = b.astype(BF16)
+        carry_a[h, cells:] = parts.astype(BF16)
     for to in range(nx):
         pl.when(to < x)(carry_copy(carry_a, carries_a, 0, to).start)
 
@@ -310,7 +319,9 @@
         def state_step(t, level):
             return decp[h, pl.ds(t, 1)] * level + src[h, frame(t)]
 
-        carry_s[h, :cells] = lax.fori_loop(0, nz, state_step, jnp.zeros((cells, ln), F32))
+        carry_s[h, :cells] = lax.fori_loop(
+            0, nz, state_step, jnp.zeros((cells, ln), F32)
+        ).astype(BF16)
         carry_s[h, cells:] = carry_a[h, cells:]
     for to in range(nx):
         pl.when(to > x)(carry_copy(carry_s, carries_s, 1, to).start)
@@ -444,11 +455,6 @@
         share_copy(o).start()
     own = pltpu.make_async_copy(share, shares.at[spot], put_sem.at[1])
     own.start()
-    for o in range(1, 2 * ny):
-        share_copy(o).wait_recv()
-    own.wait()
-    put_dinp.wait()
-
     sent(0, dec_in)
     sent(1, send_c)
     sent(2, send_i)
@@ -465,6 +471,11 @@
     @pl.loop(0, others)
     def _(i):
         xy_copy(i).wait_send()
+
+    for o in range(1, 2 * ny):
+        share_copy(o).wait_recv()
+    own.wait()
+    put_dinp.wait()
 
     for o in range(1, 2 * ny):
         share_copy(o).wait_send()
@@ -529,10 +540,10 @@
         vmem((9, states, ln), BF16),
         vmem((2, block, ln), F32),
         vmem((2, block, ln), F32),
-        vmem((2, cells + 8, ln), F32),
-        vmem((nx, 2, cells + 8, ln), F32),
-        vmem((2, cells + 8, ln), F32),
-        vmem((nx, 2, cells + 8, ln), F32),
+        vmem((2, cells + 16, ln), BF16),
+        vmem((nx, 2, cells + 16, ln), BF16),
+        vmem((2, cells + 16, ln), BF16),
+        vmem((nx, 2, cells + 16, ln), BF16),
         vmem((2, cells, ln), F32),
         vmem((2, nz, ln), F32),
         vmem((2, ny, nx, nz, 9 * ln), F32),

time: 67.9 us -> 66.7 us (0.982)
  Pallas kernels: 66.9 us -> 65.9 us
    pallas_call x1, Pallas kernels: 64.7 us -> 63.7 us  [body(): pl.pallas_call(functools.partial(kernel, nx, nz, ny, rows, ln), out_shape...]
where the time goes in v6:
time: 66.7 us; the launch traced here: 66.6 us
  Pallas kernels  65.9 us (99%)
    pallas_call x1, Pallas kernels, body(): pl.pallas_call(functools.partial(kernel, nx, nz, ny, rows, ln), out_shape...  63.7 us
    pallas_call x1, Pallas kernels, body(): pl.pallas_call(functools.partial(finish, ny, ln, wscale, dscale), out_sha...  2.2 us

profile of v6, /device:TPU:1, one launch (start us, length us, event | category | flops | bytes accessed | tf_op | source)
XLA Modules:
  0.0 66.6 jit_solution(9024196443192014264)
XLA Ops:
  0.6 63.7 %shard_map.93 = (bf16[16,32,128]{2,1,0:T(8,128)(2,1)}, f32[8,20,128]{2,1,0:T(8,128)}) custom-call(bf16[16,32,128]{2,1,0:T(8,128)(2,1)} %bitcast.14, bf16[16,32,128]{2,1,0:T(8,128)(2,1)} %bitcast.15, bf16[9,128,256]{2,1,0:T(8,128)(2,1)} %bitcast.12, bf16[9,256,128]{2,1,0:T(8,128)(2,1)} %bitcast.13, f32[1,256]{1,0:T(1,128)} %dec_hbm.1, f32[1,128]{1,0:T(1,128)} %bitcast.19), custom_call_target="tpu_custom_call" | custom-call | flops 1509949440 | bytes 4194304 | tf_op jit(solution)/shard_map/pallas_call | solution.py:574
  64.4 2.2 %shard_map.94 = (bf16[16,32,128]{2,1,0:T(8,128)(2,1)}, f32[9,4,128]{2,1,0:T(4,128)}, f32[9,4,128]{2,1,0:T(4,128)}, f32[1,256]{1,0:T(1,128)}) custom-call(bf16[16,32,128]{2,1,0:T(8,128)(2,1)} %get-tuple-element.10.dinp_hbm, f32[8,20,128]{2,1,0:T(8,128)} %get-tuple-element.11.shares_hbm), custom_call_target="tpu_custom_call" | custom-call | tf_op jit(solution)/shard_map/pallas_call | solution.py:595

commit v7 on v6

--- a/solution.py
+++ b/solution.py
@@ -483,12 +483,22 @@
 
 def finish(ny, ln, wscale, dscale, dinp_hbm, shares_hbm, out_hbm, din_ref, dout_ref, dg_ref, shares, tile, sem):
     fetch = pltpu.make_async_copy(shares_hbm, shares, sem.at[0])
-    come = pltpu.make_async_copy(dinp_hbm, tile, sem.at[1])
-    go = pltpu.make_async_copy(tile, out_hbm, sem.at[2])
-    come.start()
     fetch.start()
-    come.wait()
-    go.start()
+    size = tile.shape[0] // 4
+    parts = [pl.ds(i * size, size) for i in range(4)]
+    comes = [
+        pltpu.make_async_copy(dinp_hbm.at[part], tile.at[part], sem.at[1 + i])
+        for i, part in enumerate(parts)
+    ]
+    goes = [
+        pltpu.make_async_copy(tile.at[part], out_hbm.at[part], sem.at[5 + i])
+        for i, part in enumerate(parts)
+    ]
+    for come in comes:
+        come.start()
+    for come, go in zip(comes, goes):
+        come.wait()
+        go.start()
     fetch.wait()
     for j in range(ny):
         both = shares[2 * j] + shares[2 * j + 1]
@@ -499,7 +509,8 @@
         total += shares[s, 18:20]
     dg_ref[:, :ln] = total[:1] * dscale
     dg_ref[:, ln:] = total[1:] * dscale
-    go.wait()
+    for go in goes:
+        go.wait()
 
 
 def body(nx, inputs, cotangent, w_in, w_out, decay, skip):
@@ -602,7 +613,7 @@
         ),
         in_specs=[pl.BlockSpec(memory_space=pltpu.HBM)] * 2,
         out_specs=(pl.BlockSpec(memory_space=pltpu.HBM), whole, whole, whole),
-        scratch_shapes=[vmem((2 * ny, 20, ln), F32), vmem((rows, wide, ln), BF16), dma((3,))],
+        scratch_shapes=[vmem((2 * ny, 20, ln), F32), vmem((rows, wide, ln), BF16), dma((9,))],
         compiler_params=pltpu.CompilerParams(vmem_limit_bytes=63 * 1024 * 1024),
     )(d_inputs, shares)
 

time: 66.7 us -> 66.7 us (level)
  no operation moved by 1% of the time
where the time goes in v7:
time: 66.7 us; the launch traced here: 66.5 us
  Pallas kernels  65.9 us (99%)
    pallas_call x1, Pallas kernels, body(): pl.pallas_call(functools.partial(kernel, nx, nz, ny, rows, ln), out_shape...  63.7 us
    pallas_call x1, Pallas kernels, body(): pl.pallas_call(functools.partial(finish, ny, ln, wscale, dscale), out_sha...  2.15 us

profile of v7, /device:TPU:1, one launch (start us, length us, event | category | flops | bytes accessed | tf_op | source)
XLA Modules:
  0.0 66.5 jit_solution(15008509994530770514)
XLA Ops:
  0.6 63.7 %shard_map.93 = (bf16[16,32,128]{2,1,0:T(8,128)(2,1)}, f32[8,20,128]{2,1,0:T(8,128)}) custom-call(bf16[16,32,128]{2,1,0:T(8,128)(2,1)} %bitcast.14, bf16[16,32,128]{2,1,0:T(8,128)(2,1)} %bitcast.15, bf16[9,128,256]{2,1,0:T(8,128)(2,1)} %bitcast.12, bf16[9,256,128]{2,1,0:T(8,128)(2,1)} %bitcast.13, f32[1,256]{1,0:T(1,128)} %dec_hbm.1, f32[1,128]{1,0:T(1,128)} %bitcast.19), custom_call_target="tpu_custom_call" | custom-call | flops 1509949440 | bytes 4194304 | tf_op jit(solution)/shard_map/pallas_call | solution.py:585
  64.4 2.2 %shard_map.94 = (bf16[16,32,128]{2,1,0:T(8,128)(2,1)}, f32[9,4,128]{2,1,0:T(4,128)}, f32[9,4,128]{2,1,0:T(4,128)}, f32[1,256]{1,0:T(1,128)}) custom-call(bf16[16,32,128]{2,1,0:T(8,128)(2,1)} %get-tuple-element.10.dinp_hbm, f32[8,20,128]{2,1,0:T(8,128)} %get-tuple-element.11.shares_hbm), custom_call_target="tpu_custom_call" | custom-call | tf_op jit(solution)/shard_map/pallas_call | solution.py:606
